TPU v7x, 128 devices: a whole 4x4x4 slice. The times are simulated.
128 devices in a mesh: leaf: 16 (over z, y), row: 4 (over x), col: 2 (over core).
Axes of the slice: x: 4, y: 4, z: 4, core: 2. Of those that a mesh axis runs over, the one named last changes fastest.
Arguments:
- root_inverse: float32 [16384, 16384], P('leaf', ('row', 'col')), as said below
- blocks_one: int32 [2, 16], replicated, may hold values from 0 to 127, as said below
- blocks_two: int32 [4, 16], replicated, may hold values from 0 to 23, as said below
- blocks_three: int32 [8, 16], replicated, may hold values from 0 to 23, as said below
- blocks_four: int32 [16, 16], replicated, may hold values from 0 to 23, as said below
- update_one: float32 [2048, 2048], P('col', 'leaf'), may hold values from -0.125 to 0.125
- update_two: float32 [2048, 4096], P('col', 'leaf'), may hold values from -0.125 to 0.125
- update_three: float32 [2048, 8192], P('col', 'leaf'), may hold values from -0.125 to 0.125
- update_four: float32 [2048, 16384], P('col', 'leaf'), may hold values from -0.125 to 0.125
- pivot_one: float32 [1024, 2048], P('row', 'leaf'), as said below
- pivot_two: float32 [1024, 4096], P('row', 'leaf'), as said below
- pivot_three: float32 [1024, 8192], P('row', 'leaf'), as said below
- pivot_four: float32 [1024, 16384], P('row', 'leaf'), as said below
Outputs:
- fronts_four: float32 [16, 3072, 3072], P('leaf', 'row', 'col')
Inputs may be any that keep to these rules, and one draw needn't show every extreme that they name: `blocks_one`: row f lists 16 distinct root blocks; its entries of quarter p (entries p * 4 to (p + 1) * 4 - 1) are blocks of the root's quarter p, indices p * 4096 to (p + 1) * 4096 - 1. `blocks_two`: parent blocks are numbered in the parent front's order of positions, 6 blocks a quarter. The entries of quarter p of row f are the 2 separator blocks of the parent's quarter p in order, then distinct ancestor blocks of the parent's quarter p. `blocks_three`: as for blocks_two. `blocks_four`: as for blocks_two. `pivot_one`: each block of 1024 columns is symmetric. `pivot_two`: as for pivot_one. `pivot_three`: as for pivot_one. `pivot_four`: as for pivot_one. `root_inverse`: Symmetric.
All inputs are finite; a program needn't handle non-finite values.
Results may differ from a plain program's by a relative error of at most 0.0001.
Values sent between devices are 32-bit elements; how exact they have to be, the bound alone decides.
A program may use at most 192 MiB of HBM per device.

v0:
```python
import jax
import jax.numpy as jnp
from jax import lax
from jax.sharding import PartitionSpec as P

SEP = 1024
ANC = 2048
BS = 128


HIGH = lax.Precision.HIGHEST


def swapped(value, axis, bit):
    mask = 2**bit
    pairs = [(source, source ^ mask) for source in range(lax.axis_size(axis))]
    return lax.ppermute(value, axis, pairs)


def select_blocks(tile, row_ids, col_ids, block):
    rows, cols = tile.shape
    shaped = tile.reshape(rows // block, block, cols // block, block)
    picked = jnp.take(shaped, row_ids, axis=0)
    picked = jnp.take(picked, col_ids, axis=2)
    return picked.reshape(row_ids.shape[0] * block, col_ids.shape[0] * block)


def join_pair(mine, other, member, bit):
    lower = member >> bit & 1 == 0
    first = jnp.where(lower, mine, other)
    second = jnp.where(lower, other, mine)
    return jnp.concatenate([first, second], axis=-1)


def root_terms(root_inverse, blocks_one, quarter, eighth, leaf_pos):
    rows_here = root_inverse.shape[0] // BS
    cols_here = root_inverse.shape[1] // BS
    per_quarter = ANC // BS // 4
    terms = []
    for front in range(2):
        ids = blocks_one[front]
        own = lax.dynamic_slice_in_dim(ids, quarter * per_quarter, per_quarter)
        col_blocks = own - eighth * cols_here
        row_blocks = ids - leaf_pos * rows_here
        col_valid = (col_blocks >= 0) & (col_blocks < cols_here)
        row_valid = (row_blocks >= 0) & (row_blocks < rows_here)
        picked = select_blocks(
            root_inverse,
            jnp.clip(row_blocks, 0, rows_here - 1),
            jnp.clip(col_blocks, 0, cols_here - 1),
            BS,
        )
        valid = jnp.repeat(row_valid, BS)[:, None] & jnp.repeat(col_valid, BS)[None, :]
        terms.append(jnp.where(valid, picked, 0.0).T)
    return jnp.stack(terms)


def assemble(square, panel, upper, held, half):
    sep_q = SEP // 4
    anc_q = ANC // 4
    batch = square.shape[0]
    sep_sep = lax.dynamic_slice_in_dim(square, half * 2 * sep_q, 2 * sep_q, 2).reshape(
        batch, sep_q, 2, sep_q
    )
    anc_sep = -lax.dynamic_slice_in_dim(panel, half * 2 * sep_q, 2 * sep_q, 2).reshape(
        batch, anc_q, 2, sep_q
    )
    sep_anc = -jnp.transpose(upper, (0, 2, 1)).reshape(batch, sep_q, 2, anc_q)
    anc_anc = held.reshape(batch, anc_q, 2, anc_q)
    top = jnp.concatenate([sep_sep, sep_anc], 3)
    bottom = jnp.concatenate([anc_sep, anc_anc], 3)
    return jnp.concatenate([top, bottom], 1).reshape(batch, sep_q + anc_q, 2 * (sep_q + anc_q))


def next_held(tile, child_ids, leaf_pos, leaves, quarter, half):
    fronts = child_ids.shape[0]
    batch = max(1, fronts // leaves)
    group = max(1, leaves // fronts)
    per_quarter = ANC // BS // 4
    quarter_blocks = (SEP + ANC) // BS // 4
    ids = lax.dynamic_index_in_dim(child_ids, leaf_pos // group * batch + 0, 0, keepdims=False)
    row_ids = (
        lax.dynamic_slice_in_dim(ids, quarter * per_quarter, per_quarter) - quarter * quarter_blocks
    )
    col_ids = (
        lax.dynamic_slice_in_dim(ids, half * 2 * per_quarter, 2 * per_quarter)
        - half * 2 * quarter_blocks
    )
    picked = [select_blocks(tile[0 // 2], row_ids, col_ids, BS)]
    return jnp.stack(picked)


def shards(
    root_inverse,
    blocks_one,
    blocks_two,
    blocks_three,
    blocks_four,
    update_one,
    update_two,
    update_three,
    update_four,
    pivot_one,
    pivot_two,
    pivot_three,
    pivot_four,
):
    leaves = lax.axis_size("leaf")
    leaf_pos = lax.axis_index("leaf")
    quarter = lax.axis_index("row")
    half = lax.axis_index("col")
    terms = root_terms(root_inverse, blocks_one, quarter, quarter * 2 + half, leaf_pos)
    front_one = leaf_pos // (leaves // 2)
    halves = lax.psum_scatter(terms, "col", scatter_dimension=2, tiled=True)
    total = lax.psum(halves, "leaf")
    held = lax.dynamic_index_in_dim(total, front_one, 0, keepdims=False)
    held = held[None]
    levels = (
        (update_one, pivot_one, blocks_two),
        (update_two, pivot_two, blocks_three),
        (update_three, pivot_three, blocks_four),
        (update_four, pivot_four, None),
    )
    tile = None
    for depth, (update, pivot, child_ids) in enumerate(levels):
        fronts = 2 ** (depth + 1)
        batch = max(1, fronts // leaves)
        group = max(1, leaves // fronts)
        member = leaf_pos % group
        bits = group.bit_length() - 1
        width = update.shape[1] // batch
        cols_update = update.reshape(ANC // 2, batch, width)
        cols_pivot = pivot.reshape(SEP // 4, batch, width)
        part = jnp.einsum(
            "nij,jnk->nik", held, cols_update, precision=HIGH, preferred_element_type=jnp.float32
        )
        panel = lax.psum(part, "col")
        for bit in range(bits):
            panel = join_pair(panel, swapped(panel, "leaf", bit), member, bit)
        crossed = lax.all_to_all(panel, "row", split_axis=2, concat_axis=1, tiled=True)
        upper = lax.dynamic_slice_in_dim(crossed, half * (ANC // 2), ANC // 2, 1)
        inner = jnp.einsum(
            "naj,ank->njk", upper, cols_update, precision=HIGH, preferred_element_type=jnp.float32
        )
        square = lax.psum(inner, "col") + jnp.transpose(cols_pivot, (1, 0, 2))
        for bit in range(bits):
            square = join_pair(square, swapped(square, "leaf", bit), member, bit)
        tile = assemble(square, panel, upper, held, half)
        if child_ids is not None:
            held = next_held(tile, child_ids, leaf_pos, leaves, quarter, half)
    return tile


def solution(mesh):
    placed = (
        P("leaf", ("row", "col")),
        P(),
        P(),
        P(),
        P(),
        P("col", "leaf"),
        P("col", "leaf"),
        P("col", "leaf"),
        P("col", "leaf"),
        P("row", "leaf"),
        P("row", "leaf"),
        P("row", "leaf"),
        P("row", "leaf"),
    )
    return jax.shard_map(
        shards, mesh=mesh, in_specs=placed, out_specs=P("leaf", "row", "col"), check_vma=False
    )
```

profile of v0, /device:TPU:1, one launch (start us, length us, event | category | flops | bytes accessed | tf_op | source)
XLA Modules:
  0.0 1048.5 jit_solution(18406596428135236489)
XLA Ops:
  9.1 8.6 copy.167
  17.7 10.9 %gather_fusion.2 = f32[16,128,16,128]{3,2,1,0:T(8,128)} fusion(f32[8,128,16,128]{3,2,1,0:T(8,128)} %bitcast.196, s32[1024]{0:T(1024)S(1)} %pad_clamp_fusion.7), kind=kCustom, calls=%fused_computation.4.clone | custom fusion | bytes 33554496 | tf_op jit(solution)/shard_map/jit(_take)/gather | solution.py:23
  28.7 11.0 %gather_fusion = f32[16,128,16,128]{3,2,1,0:T(8,128)} fusion(f32[8,128,16,128]{3,2,1,0:T(8,128)} %bitcast.197, s32[1024]{0:T(1024)S(1)} %pad_clamp_fusion.9), kind=kCustom, calls=%fused_computation.clone | custom fusion | bytes 33554496 | tf_op jit(solution)/shard_map/jit(_take)/gather | solution.py:23
  39.7 17.9 %broadcast_select_fusion = (f32[16,128,16,128]{3,2,1,0:T(8,128)S(1)}, f32[16,128,16,128]{3,2,1,0:T(8,128)}) fusion(f32[16,128,16,128]{3,2,1,0:T(8,128)} %gather_fusion.2, pred[16]{0:T(512)(128)(4,1)S(1)} %get-tuple-element.57, f32[16,128,16,128]{3,2,1,0:T(8,128)} %gather_fusion, pred[16]{0:T(512)(128)(4,1)S(1)} %get-tuple-element.23), kind=kLoop, calls=%fused_computation.11 | loop fusion | flops 8388608 | bytes 67108896 | tf_op jit(solution)/shard_map/jit(_take)/select_n | solution.py:23
  57.6 7.9 copy.125
  65.5 8.6 gather_fusion.3
  79.0 5.4 copy.126
  84.5 15.8 %copy.123 = f32[16,128,16,128]{3,1,2,0:T(8,128)} copy(f32[16,128,16,128]{3,2,1,0:T(8,128)} %get-tuple-element.64) | data formatting | bytes 33554432 | tf_op jit(solution)/shard_map/jit(_take)/select_n | solution.py:23
  100.3 8.6 gather_fusion.1
  113.8 5.6 copy.124
  130.3 23.9 %reduce-scatter.2.cloned.1.call-done = f32[2,512,1024]{2,1,0:T(8,128)} async-done(((f32[2,512,2048]{2,1,0:T(8,128)}), f32[2,512,1024]{2,1,0:T(8,128)}) %reduce-scatter.2.cloned.1.call-update) | async-done | bytes 4194320 | tf_op jit(solution)/shard_map/reduce_scatter | solution.py:114
  154.3 108.0 %all-reduce.10.cloned.1.call-done = f32[2,512,1024]{2,1,0:T(8,128)} async-done(((f32[2,512,1024]{2,1,0:T(8,128)}), f32[2,512,1024]{2,1,0:T(8,128)}) %all-reduce.10.cloned.1.call-update) | async-done | bytes 4194320 | tf_op jit(solution)/shard_map/psum | solution.py:115
  267.9 24.3 %all-reduce.12.cloned.1.call-done = f32[1,512,128]{2,1,0:T(8,128)} async-done(((f32[1,512,128]{2,1,0:T(8,128)}), f32[1,512,128]{2,1,0:T(8,128)}) %all-reduce.12.cloned.1.call-update) | async-done | bytes 262160 | tf_op jit(solution)/shard_map/psum | solution.py:137
  293.6 6.6 collective-permute-done
  304.8 11.3 %collective-permute-done.1 = f32[1,512,256]{2,1,0:T(8,128)S(1)} collective-permute-done((f32[1,512,256]{2,1,0:T(8,128)}, f32[1,512,256]{2,1,0:T(8,128)S(1)}, u32[]{:S(2)}, u32[]{:S(2)}) %collective-permute-start.1) | collective-permute-done | bytes 524320 | tf_op jit(solution)/shard_map/ppermute | solution.py:17
  318.6 21.4 %collective-permute-done.2 = f32[1,512,512]{2,1,0:T(8,128)} collective-permute-done((f32[1,512,512]{2,1,0:T(8,128)S(1)}, f32[1,512,512]{2,1,0:T(8,128)}, u32[]{:S(2)}, u32[]{:S(2)}) %collective-permute-start.2) | collective-permute-done | bytes 1048608 | tf_op jit(solution)/shard_map/ppermute | solution.py:17
  344.3 6.0 copy.127
  354.9 23.5 %all-to-all-done = f32[1,512,1024]{1,0,2:T(1,128)} async-done(((f32[1,512,1024]{1,0,2:T(1,128)}), f32[1,512,1024]{1,0,2:T(1,128)}, u32[]{:S(2)}, u32[]{:S(2)}) %all-to-all-start) | async-done | bytes 2097184 | tf_op jit(solution)/shard_map/all_to_all | solution.py:140
  388.4 26.7 %all-reduce.14.cloned.1.call-done = f32[1,256,128]{2,1,0:T(8,128)} async-done(((f32[1,256,128]{2,1,0:T(8,128)}), f32[1,256,128]{2,1,0:T(8,128)}) %all-reduce.14.cloned.1.call-update) | async-done | bytes 131088 | tf_op jit(solution)/shard_map/psum | solution.py:145
  425.1 5.7 collective-permute-done.4
  453.9 6.6 reshape_squeeze_reshape.9
  460.5 5.9 copy.132
  486.4 28.5 %all-reduce.16.cloned.1.call-done = f32[1,512,256]{2,1,0:T(8,128)} async-done(((f32[1,512,256]{2,1,0:T(8,128)}), f32[1,512,256]{2,1,0:T(8,128)}) %all-reduce.16.cloned.1.call-update) | async-done | bytes 524304 | tf_op jit(solution)/shard_map/psum | solution.py:137
  516.2 12.2 %collective-permute-done.6 = f32[1,512,256]{2,1,0:T(8,128)S(1)} collective-permute-done((f32[1,512,256]{2,1,0:T(8,128)}, f32[1,512,256]{2,1,0:T(8,128)S(1)}, u32[]{:S(2)}, u32[]{:S(2)}) %collective-permute-start.6) | collective-permute-done | bytes 524320 | tf_op jit(solution)/shard_map/ppermute | solution.py:17
  533.4 22.4 %collective-permute-done.7 = f32[1,512,512]{2,1,0:T(8,128)} collective-permute-done((f32[1,512,512]{2,1,0:T(8,128)S(1)}, f32[1,512,512]{2,1,0:T(8,128)}, u32[]{:S(2)}, u32[]{:S(2)}) %collective-permute-start.7) | collective-permute-done | bytes 1048608 | tf_op jit(solution)/shard_map/ppermute | solution.py:17
  560.0 6.0 copy.134
  566.1 28.1 %all_to_all.72 = f32[1,512,1024]{1,0,2:T(1,128)S(1)} all-to-all(f32[1,512,1024]{1,0,2:T(1,128)} %copy.134), channel_id=1, replica_groups=mesh['leaf'=16,'row'=4,'col'=2] {'row'}, dimensions={2} | all-to-all | bytes 4194304 | tf_op jit(solution)/shard_map/all_to_all | solution.py:140
  602.8 26.4 %all-reduce.18.cloned.1.call-done = f32[1,256,256]{2,1,0:T(8,128)} async-done(((f32[1,256,256]{2,1,0:T(8,128)}), f32[1,256,256]{2,1,0:T(8,128)}) %all-reduce.18.cloned.1.call-update) | async-done | bytes 262160 | tf_op jit(solution)/shard_map/psum | solution.py:145
  632.4 5.7 collective-permute-done.8
  661.7 13.1 %maximum_maximum_fusion.1 = f32[1,768,2,768]{3,2,1,0:T(2,128)} fusion(f32[1,512,2,512]{3,2,1,0:T(2,128)} %reshape_stack_reshape.9, f32[1,512,2,256]{3,2,1,0:T(2,128)S(1)} %neg.133, f32[1,256,2,512]{3,2,1,0:T(2,128)} %copy.138, f32[1,256,2,256]{3,2,1,0:T(2,128)} %copy.137), kind=kLoop, calls=%fused_computation.14 | loop fusion | flops 3538944 | bytes 9437184 | tf_op jit(solution)/shard_map/concatenate | solution.py:72
  674.7 7.8 reshape.403
  682.5 6.4 copy.141
  710.8 28.1 %all-reduce.20.cloned.1.call-done = f32[1,512,512]{2,1,0:T(8,128)} async-done(((f32[1,512,512]{2,1,0:T(8,128)}), f32[1,512,512]{2,1,0:T(8,128)}) %all-reduce.20.cloned.1.call-update) | async-done | bytes 1048592 | tf_op jit(solution)/shard_map/psum | solution.py:137
  740.2 23.5 %collective-permute-done.10 = f32[1,512,512]{2,1,0:T(8,128)} collective-permute-done((f32[1,512,512]{2,1,0:T(8,128)}, f32[1,512,512]{2,1,0:T(8,128)}, u32[]{:S(2)}, u32[]{:S(2)}) %collective-permute-start.10) | collective-permute-done | bytes 1048608 | tf_op jit(solution)/shard_map/ppermute | solution.py:17
  768.0 6.0 copy.143
  774.1 28.8 %all_to_all.73 = f32[1,512,1024]{1,0,2:T(1,128)S(1)} all-to-all(f32[1,512,1024]{1,0,2:T(1,128)} %copy.143), channel_id=1, replica_groups=mesh['leaf'=16,'row'=4,'col'=2] {'row'}, dimensions={2} | all-to-all | bytes 4194304 | tf_op jit(solution)/shard_map/all_to_all | solution.py:140
  812.2 25.4 %all-reduce.22.cloned.1.call-done = f32[1,256,512]{2,1,0:T(8,128)} async-done(((f32[1,256,512]{2,1,0:T(8,128)}), f32[1,256,512]{2,1,0:T(8,128)}) %all-reduce.22.cloned.1.call-update) | async-done | bytes 524304 | tf_op jit(solution)/shard_map/psum | solution.py:145
  859.6 13.1 %maximum_maximum_fusion.2 = f32[1,768,2,768]{3,2,1,0:T(2,128)} fusion(f32[1,512,2,512]{3,2,1,0:T(2,128)} %reshape_stack_reshape.10, f32[1,512,2,256]{3,2,1,0:T(2,128)S(1)} %neg.138, f32[1,256,2,512]{3,2,1,0:T(2,128)} %copy.147, f32[1,256,2,256]{3,2,1,0:T(2,128)} %copy.146), kind=kLoop, calls=%fused_computation.15 | loop fusion | flops 3538944 | bytes 9437184 | tf_op jit(solution)/shard_map/concatenate | solution.py:72
  872.6 7.8 reshape.404
  880.4 6.4 copy.150
  904.0 8.3 fusion.13
  912.4 29.1 %all-reduce.24.cloned.1.call-done = f32[1,512,1024]{2,1,0:T(8,128)} async-done(((f32[1,512,1024]{2,1,0:T(8,128)}), f32[1,512,1024]{2,1,0:T(8,128)}) %all-reduce.24.cloned.1.call-update) | async-done | bytes 2097168 | tf_op jit(solution)/shard_map/psum | solution.py:137
  941.5 6.0 copy.152
  947.5 30.2 %all_to_all.74 = f32[1,512,1024]{1,0,2:T(1,128)S(1)} all-to-all(f32[1,512,1024]{1,0,2:T(1,128)} %copy.152), channel_id=1, replica_groups=mesh['leaf'=16,'row'=4,'col'=2] {'row'}, dimensions={2} | all-to-all | bytes 4194304 | tf_op jit(solution)/shard_map/all_to_all | solution.py:140
  982.1 7.1 convolution_bitcast_fusion
  1001.3 13.9 %all-reduce.26.cloned.1.call-done = f32[1,256,1024]{2,1,0:T(8,128)} async-done(((f32[1,256,1024]{2,1,0:T(8,128)}), f32[1,256,1024]{2,1,0:T(8,128)}) %all-reduce.26.cloned.1.call-update) | async-done | bytes 1048592 | tf_op jit(solution)/shard_map/psum | solution.py:145
  1021.3 13.1 %maximum_maximum_fusion.3 = f32[1,768,2,768]{3,2,1,0:T(2,128)} fusion(f32[1,512,2,512]{3,2,1,0:T(2,128)} %reshape_stack_reshape.11, f32[1,512,2,256]{3,2,1,0:T(2,128)S(1)} %neg.143, f32[1,256,2,512]{3,2,1,0:T(2,128)} %copy.156, f32[1,256,2,256]{3,2,1,0:T(2,128)} %copy.155), kind=kLoop, calls=%fused_computation.16 | loop fusion | flops 3538944 | bytes 9437184 | tf_op jit(solution)/shard_map/concatenate | solution.py:72
  1034.4 7.0 reshape.292
  (195 shorter events, 253.4 us)
Async XLA Ops:
  6.5 699.6 %copy-start = (f32[1024,512]{1,0:T(8,128)S(1)}, f32[1024,512]{1,0:T(8,128)}, u32[]{:S(2)}) copy-start(f32[1024,512]{1,0:T(8,128)} %param.28) | copy-start | bytes 6291460
  6.5 147.6 %reduce-scatter.2.cloned.1.call-start = ((), (), s32[]{:S(2)}) async-start(), calls=%async_computation.5 | async-start | bytes 12582912 | tf_op jit(solution)/shard_map/reduce_scatter | solution.py:114
  119.6 4.5 copy-start.5
  130.2 132.1 %all-reduce.10.cloned.1.call-start = ((), (), s32[]{:S(2)}) async-start(), calls=%async_computation.6 | async-start | bytes 8388608 | tf_op jit(solution)/shard_map/psum | solution.py:115
  154.2 111.2 %copy-start.17 = (f32[1024,128]{1,0:T(8,128)S(1)}, f32[1024,128]{1,0:T(8,128)}, u32[]{:S(2)}) copy-start(f32[1024,128]{1,0:T(8,128)} %param.26) | copy-start | bytes 1572868
  154.2 138.1 %all-reduce.12.cloned.1.call-start = ((), (), s32[]{:S(2)}) async-start(), calls=%async_computation.7 | async-start | bytes 524288 | tf_op jit(solution)/shard_map/psum | solution.py:137
  264.1 1.3 copy-start.2
  292.3 7.9 collective-permute-start
  302.0 14.1 %collective-permute-start.1 = (f32[1,512,256]{2,1,0:T(8,128)}, f32[1,512,256]{2,1,0:T(8,128)S(1)}, u32[]{:S(2)}, u32[]{:S(2)}) collective-permute-start(f32[1,512,256]{2,1,0:T(8,128)} %pad_maximum_fusion.6), channel_id=1, source_target_pairs={{0,16},{8,24},{16,0},{24,8},{32,48},{40,56},{48,32},{56,40},{64,80... | collective-permute-start | bytes 1572872 | tf_op jit(solution)/shard_map/ppermute | solution.py:17
  316.2 0.8 copy-start.10
  316.2 1.0 copy-start.11
  317.2 22.9 %collective-permute-start.2 = (f32[1,512,512]{2,1,0:T(8,128)S(1)}, f32[1,512,512]{2,1,0:T(8,128)}, u32[]{:S(2)}, u32[]{:S(2)}) collective-permute-start(f32[1,512,512]{2,1,0:T(8,128)S(1)} %pad_maximum_fusion.4), channel_id=1, source_target_pairs={{0,32},{8,40},{16,48},{24,56},{32,0},{40,8},{48,16},{56,24},{64,96... | collective-permute-start | bytes 3145736 | tf_op jit(solution)/shard_map/ppermute | solution.py:17
  341.8 1.0 copy-start.7
  350.4 28.0 %all-to-all-start = ((f32[1,512,1024]{1,0,2:T(1,128)}), f32[1,512,1024]{1,0,2:T(1,128)}, u32[]{:S(2)}, u32[]{:S(2)}) async-start(f32[1,512,1024]{1,0,2:T(1,128)} %copy.127), calls=%async_computation.1 | async-start | bytes 4194304 | tf_op jit(solution)/shard_map/all_to_all | solution.py:140
  354.8 60.2 %all-reduce.14.cloned.1.call-start = ((), (), s32[]{:S(2)}) async-start(), calls=%async_computation.8 | async-start | bytes 262144 | tf_op jit(solution)/shard_map/psum | solution.py:145
  381.5 33.5 %copy-start.20 = (f32[256,128]{1,0:T(8,128)S(1)}, f32[256,128]{1,0:T(8,128)}, u32[]{:S(2)}) copy-start(f32[256,128]{1,0:T(8,128)} %param.30) | copy-start | bytes 393220
  381.5 43.5 %copy-start.21 = (s32[4,16]{1,0:T(4,128)S(1)}, s32[4,16]{1,0:T(4,128)}, u32[]{:S(2)}) copy-start(s32[4,16]{1,0:T(4,128)} %param.23) | copy-start | bytes 772
  388.3 126.5 %all-reduce.16.cloned.1.call-start = ((), (), s32[]{:S(2)}) async-start(), calls=%async_computation.9 | async-start | bytes 1048576 | tf_op jit(solution)/shard_map/psum | solution.py:137
  416.0 5.0 collective-permute-start.3
  421.0 4.1 copy-start.18
  421.7 9.1 collective-permute-start.4
  431.8 0.7 copy-start.15
  433.4 11.8 %collective-permute-start.5 = (f32[1,256,512]{2,1,0:T(8,128)}, f32[1,256,512]{2,1,0:T(8,128)}, u32[]{:S(2)}, u32[]{:S(2)}) collective-permute-start(f32[1,256,512]{2,1,0:T(8,128)} %pad_maximum_fusion.7), channel_id=1, source_target_pairs={{0,32},{8,40},{16,48},{24,56},{32,0},{40,8},{48,16},{56,24},{64,96... | collective-permute-start | bytes 1572872 | tf_op jit(solution)/shard_map/ppermute | solution.py:17
  481.1 2.6 copy-start.14
  482.3 1.3 copy-start.1
  486.4 142.8 %all-reduce.18.cloned.1.call-start = ((), (), s32[]{:S(2)}) async-start(), calls=%async_computation.10 | async-start | bytes 524288 | tf_op jit(solution)/shard_map/psum | solution.py:145
  514.9 13.5 %collective-permute-start.6 = (f32[1,512,256]{2,1,0:T(8,128)}, f32[1,512,256]{2,1,0:T(8,128)S(1)}, u32[]{:S(2)}, u32[]{:S(2)}) collective-permute-start(f32[1,512,256]{2,1,0:T(8,128)} %all-reduce.16.cloned.1.call-done), channel_id=1, source_target_pairs={{0,8},{8,0},{16,24},{24,16},{32,40},{40,32},{48,56},{56,48},{64,72... | collective-permute-start | bytes 1572872 | tf_op jit(solution)/shard_map/ppermute | solution.py:17
  529.5 0.8 copy-start.12
  529.5 1.0 copy-start.13
  530.5 25.3 %collective-permute-start.7 = (f32[1,512,512]{2,1,0:T(8,128)S(1)}, f32[1,512,512]{2,1,0:T(8,128)}, u32[]{:S(2)}, u32[]{:S(2)}) collective-permute-start(f32[1,512,512]{2,1,0:T(8,128)S(1)} %pad_maximum_fusion.5), channel_id=1, source_target_pairs={{0,16},{8,24},{16,0},{24,8},{32,48},{40,56},{48,32},{56,40},{64,80... | collective-permute-start | bytes 3145736 | tf_op jit(solution)/shard_map/ppermute | solution.py:17
  557.5 1.0 copy-start.8
  602.7 136.2 %all-reduce.20.cloned.1.call-start = ((), (), s32[]{:S(2)}) async-start(), calls=%async_computation.11 | async-start | bytes 2097152 | tf_op jit(solution)/shard_map/psum | solution.py:137
  630.2 2.2 copy-start.19
  630.3 7.9 collective-permute-start.8
  639.2 0.7 copy-start.16
  640.8 14.7 %collective-permute-start.9 = (f32[1,256,512]{2,1,0:T(8,128)}, f32[1,256,512]{2,1,0:T(8,128)}, u32[]{:S(2)}, u32[]{:S(2)}) collective-permute-start(f32[1,256,512]{2,1,0:T(8,128)} %pad_maximum_fusion.8), channel_id=1, source_target_pairs={{0,16},{8,24},{16,0},{24,8},{32,48},{40,56},{48,32},{56,40},{64,80... | collective-permute-start | bytes 1572872 | tf_op jit(solution)/shard_map/ppermute | solution.py:17
  704.8 1.3 copy-start.3
  710.8 126.8 %all-reduce.22.cloned.1.call-start = ((), (), s32[]{:S(2)}) async-start(), calls=%async_computation.12 | async-start | bytes 1048576 | tf_op jit(solution)/shard_map/psum | solution.py:145
  738.9 24.9 %collective-permute-start.10 = (f32[1,512,512]{2,1,0:T(8,128)}, f32[1,512,512]{2,1,0:T(8,128)}, u32[]{:S(2)}, u32[]{:S(2)}) collective-permute-start(f32[1,512,512]{2,1,0:T(8,128)} %all-reduce.20.cloned.1.call-done), channel_id=1, source_target_pairs={{0,8},{8,0},{16,24},{24,16},{32,40},{40,32},{48,56},{56,48},{64,72... | collective-permute-start | bytes 3145736 | tf_op jit(solution)/shard_map/ppermute | solution.py:17
  765.5 1.0 copy-start.9
  811.4 130.1 %all-reduce.24.cloned.1.call-start = ((), (), s32[]{:S(2)}) async-start(), calls=%async_computation.13 | async-start | bytes 4194304 | tf_op jit(solution)/shard_map/psum | solution.py:137
  839.6 13.6 %collective-permute-start.11 = (f32[1,256,512]{2,1,0:T(8,128)}, f32[1,256,512]{2,1,0:T(8,128)}, u32[]{:S(2)}, u32[]{:S(2)}) collective-permute-start(f32[1,256,512]{2,1,0:T(8,128)} %bitcast_add_fusion), channel_id=1, source_target_pairs={{0,8},{8,0},{16,24},{24,16},{32,40},{40,32},{48,56},{56,48},{64,72... | collective-permute-start | bytes 1572872 | tf_op jit(solution)/shard_map/ppermute | solution.py:17
  901.4 2.6 copy-start.6
  902.7 1.3 copy-start.4
  912.3 102.8 %all-reduce.26.cloned.1.call-start = ((), (), s32[]{:S(2)}) async-start(), calls=%async_computation.14 | async-start | bytes 2097152 | tf_op jit(solution)/shard_map/psum | solution.py:145
Sparse Core Ops, SparseCore 0:
  130.3 23.8 reduce-scatter.1
  157.9 104.3 all-reduce.9
  268.0 24.1 all-reduce.11
  388.4 26.5 all-reduce.13
  486.5 28.3 all-reduce.15
  602.8 26.2 all-reduce.17
  710.9 27.9 all-reduce.19
  811.5 26.0 all-reduce.21
  912.5 28.9 all-reduce.23
  989.4 25.7 all-reduce.25
where the time goes:
time: 1060 us; the launch traced here: 1050 us
  waiting for transfers between devices  473 us (45%)
  local copies, waits for them, and re-layouts  260 us (25%)
  other arithmetic  149 us (14%)
  blocking collectives  87.1 us (8%)
  matrix products  37.1 us (4%)
  starting transfers between devices  27.7 us (3%)
  between operations  14.2 us (1%)
    ppermute x12, waiting for transfers between devices, swapped(): return lax.ppermute(value, axis, pairs)  115 us
    psum x4, waiting for transfers between devices, shards(): panel = lax.psum(part, 'col')  110 us
    psum x1, waiting for transfers between devices, shards(): total = lax.psum(halves, 'leaf')  108 us
    psum x4, waiting for transfers between devices, shards(): square = lax.psum(inner, 'col') + jnp.transpose(cols_pivot, (1, 0, 2))  92.4 us
    all_to_all x3, blocking collectives, shards(): lax.all_to_all(panel, 'row', split_axis=2, concat_axis=1, tiled=True)  87.1 us
    concatenate x4, other arithmetic, assemble(): jnp.concatenate([top, bottom], 1)  43.7 us
    another operation x6, local copies, waits for them, and re-layouts, select_blocks(): shaped = tile.reshape(rows // block, block, cols // block, block)  40.9 us
    gather x5, local copies, waits for them, and re-layouts, select_blocks(): picked = jnp.take(shaped, row_ids, axis=0)  36.1 us
  transfers between devices with their start and end apart: 23, of which 22 were waited for; matrix products, arithmetic and copies ran while one was open for 4% of the time, Pallas kernels for 0%

commit v1 on v0

v1 whole, which is shorter than its diff:
```python
import functools

import jax
import jax.numpy as jnp
from jax import lax
from jax.experimental import pallas as pl
from jax.experimental.pallas import tpu as pltpu
from jax.sharding import Mesh, PartitionSpec as P

SEP = 1024
ANC = 2048
BS = 128
AXES = ("za", "zb", "ya", "yb", "row", "col")
MESH = pl.DeviceIdType.MESH
VMEM = pl.BlockSpec(memory_space=pltpu.VMEM)
SMEM = pl.BlockSpec(memory_space=pltpu.SMEM)
ANY = pl.BlockSpec(memory_space=pl.ANY)
F32 = jnp.float32
BF16 = jnp.bfloat16


def place():
    z = lax.axis_index("za") * 2 + lax.axis_index("zb")
    y = lax.axis_index("ya") * 2 + lax.axis_index("yb")
    return z, y, lax.axis_index("row"), lax.axis_index("col")


def device(z, y, x, c):
    return (z // 2, z % 2, y // 2, y % 2, x, c)


def halves(value):
    high = value.astype(BF16)
    return high, (value - high.astype(F32)).astype(BF16)


def dot(a, b):
    return jnp.dot(a, b, preferred_element_type=F32)


def pick_kernel(ids_ref, root_ref, out_ref, blocks, sems):
    z, y, x, c = place()

    def source(f, j, i):
        row = ids_ref[f, z * 4 + i] - (z * 4 + y) * 8
        col = ids_ref[f, x * 4 + j] - (x * 2 + c) * 16
        valid = (row >= 0) & (row < 8) & (col >= 0) & (col < 16)
        return jnp.clip(row, 0, 7), jnp.clip(col, 0, 15), valid

    def copy(n, row, col):
        return pltpu.make_async_copy(
            root_ref.at[
                pl.ds(pl.multiple_of(row * BS, BS), BS), pl.ds(pl.multiple_of(col * BS, BS), BS)
            ],
            blocks.at[n],
            sems.at[n],
        )

    triples = [(f, j, i) for f in range(2) for j in range(4) for i in range(4)]
    for n, (f, j, i) in enumerate(triples):
        row, col, _ = source(f, j, i)
        copy(n, row, col).start()
    for n, (f, j, i) in enumerate(triples):
        row, col, valid = source(f, j, i)
        copy(n, row, col).wait()
        at = i % 2 * 2 + i // 2
        out_ref[f, j, at] = jnp.where(valid, blocks[n].T, 0.0)


def pick(ids, root):
    return pl.pallas_call(
        pick_kernel,
        out_shape=jax.ShapeDtypeStruct((2, 4, 4, BS, BS), F32),
        in_specs=[SMEM, ANY],
        out_specs=VMEM,
        scratch_shapes=[pltpu.VMEM((32, BS, BS), F32), pltpu.SemaphoreType.DMA((32,))],
        compiler_params=pltpu.CompilerParams(vmem_limit_bytes=32 * 2**20),
        name="pick",
    )(ids, root)


def spread_kernel(m_ref, out_ref, core_in, mine, y_in, ready, core_s, core_r, ys, yr, hs, hr):
    z, y, x, c = place()
    barrier = pltpu.get_barrier_semaphore()

    def signal(dev):
        pl.semaphore_signal(barrier, inc=1, device_id=dev, device_id_type=MESH)

    mine_f = z // 2
    signal(device(z, y, x, 1 - c))
    for d in range(1, 4):
        signal(device(z, (y + d) % 4, x, c))
    for p in range(4):
        for r in range(2):
            j = 2 * r + c

            @pl.when(jnp.logical_not((p == z) & (j == y) & (mine_f == c)))
            def _():
                signal(device(p, j, x, mine_f))

    own = (mine_f == c) & (y % 2 == c)
    pl.semaphore_wait(barrier, jnp.where(own, 11, 12))

    core = pltpu.make_async_remote_copy(
        src_ref=m_ref.at[1 - c],
        dst_ref=core_in,
        send_sem=core_s,
        recv_sem=core_r,
        device_id=device(z, y, x, 1 - c),
        device_id_type=MESH,
    )
    core.start()
    core.wait()
    mine[...] = m_ref[c] + core_in[...]

    def y_copy(d):
        to = (y + d) % 4
        return pltpu.make_async_remote_copy(
            src_ref=mine.at[to],
            dst_ref=y_in.at[d - 1],
            send_sem=ys.at[d - 1],
            recv_sem=yr.at[d - 1],
            device_id=device(z, to, x, c),
            device_id_type=MESH,
        )

    for d in (2, 1, 3):
        y_copy(d).start()
    for d in (1, 3, 2):
        y_copy(d).wait()
    ready[...] = mine[y] + y_in[0] + y_in[1] + y_in[2]

    def h_copy(k, d):
        return pltpu.make_async_remote_copy(
            src_ref=ready,
            dst_ref=out_ref.at[y // 2, pl.ds(4 * z, 4)],
            send_sem=hs.at[k * 4 + d],
            recv_sem=hr.at[z * 2 + y // 2],
            device_id=device(2 * c + k, (y + d) % 4, x, y % 2),
            device_id_type=MESH,
        )

    def to_self(k, d):
        return (2 * c + k == z) & (d == 0) & (y % 2 == c)

    for d in (2, 1, 3, 0):
        for k in range(2):
            if d == 0:

                @pl.when(jnp.logical_not(to_self(k, d)))
                def _():
                    h_copy(k, d).start()

                @pl.when(to_self(k, d))
                def _():
                    out_ref[y // 2, pl.ds(4 * z, 4)] = ready[...]

            else:
                h_copy(k, d).start()
    for d in (2, 1, 3, 0):
        for k in range(2):
            if d == 0:

                @pl.when(jnp.logical_not(to_self(k, d)))
                def _():
                    h_copy(k, d).wait_send()

            else:
                h_copy(k, d).wait_send()
    for p in range(4):
        for r in range(2):

            @pl.when(jnp.logical_not((p == z) & (2 * r + c == y) & (mine_f == c)))
            def _():
                pltpu.make_async_remote_copy(
                    src_ref=ready,
                    dst_ref=out_ref.at[r, pl.ds(4 * p, 4)],
                    send_sem=hs.at[0],
                    recv_sem=hr.at[p * 2 + r],
                    device_id=device(z, y, x, 1 - c),
                    device_id_type=MESH,
                ).wait_recv()


def spread(picked):
    return pl.pallas_call(
        spread_kernel,
        out_shape=jax.ShapeDtypeStruct((2, 16, BS, BS), F32),
        in_specs=[VMEM],
        out_specs=VMEM,
        scratch_shapes=[
            pltpu.VMEM((4, 4, BS, BS), F32),
            pltpu.VMEM((4, 4, BS, BS), F32),
            pltpu.VMEM((3, 4, BS, BS), F32),
            pltpu.VMEM((4, BS, BS), F32),
            pltpu.SemaphoreType.DMA,
            pltpu.SemaphoreType.DMA,
            pltpu.SemaphoreType.DMA((3,)),
            pltpu.SemaphoreType.DMA((3,)),
            pltpu.SemaphoreType.DMA((8,)),
            pltpu.SemaphoreType.DMA((8,)),
        ],
        compiler_params=pltpu.CompilerParams(
            collective_id=0, has_side_effects=True, vmem_limit_bytes=48 * 2**20
        ),
        name="spread",
    )(picked)


def level_kernel(
    last, sel_ref, h_ref, u_ref, v_ref, out_ref,
    hq, pq, uhi, ulo, hs, st, ptl, acc, xin, xs_s, xs_r, ss, rs, hx_s, hx_r, px_s, px_r,
):
    z, y, q, c = place()
    e = 2 * q + c
    partner = device(z, y, q, 1 - c)
    barrier = pltpu.get_barrier_semaphore()
    for t in range(8):

        @pl.when(t != e)
        def _():
            pl.semaphore_signal(
                barrier, inc=1, device_id=device(z, y, t // 2, t % 2), device_id_type=MESH
            )

    def split_u(b, carry):
        m = b // 2
        src = 4 * (m // 2) + 2 * (b % 2) + m % 2
        hi, lo = halves(u_ref[pl.ds(pl.multiple_of(src * BS, BS), BS), :])
        at = pl.ds(pl.multiple_of(b * BS, BS), BS)
        uhi[at, :] = hi
        ulo[at, :] = lo
        return carry

    lax.fori_loop(0, 16, split_u, 0)
    for r in range(2):
        for b in range(16):
            value = h_ref[r, b]
            hi, lo = halves(value)
            hs[r * BS : r * BS + BS, b * BS : b * BS + BS] = hi
            hs[256 + r * BS : 256 + r * BS + BS, b * BS : b * BS + BS] = lo
            hq[2 * r + c, b] = value
    pl.semaphore_wait(barrier, 7)

    def core_copy(ref, r, s_sem, r_sem):
        return pltpu.make_async_remote_copy(
            src_ref=ref.at[2 * r + c],
            dst_ref=ref.at[2 * r + c],
            send_sem=s_sem.at[r],
            recv_sem=r_sem.at[r],
            device_id=partner,
            device_id_type=MESH,
        )

    def core_arrived(ref, r, s_sem, r_sem):
        return pltpu.make_async_remote_copy(
            src_ref=ref.at[2 * r + 1 - c],
            dst_ref=ref.at[2 * r + 1 - c],
            send_sem=s_sem.at[r],
            recv_sem=r_sem.at[r],
            device_id=partner,
            device_id_type=MESH,
        )

    for r in range(2):
        core_copy(hq, r, hx_s, hx_r).start()

    def piece(to):
        return pltpu.make_async_remote_copy(
            src_ref=st.at[to],
            dst_ref=ptl.at[pl.ds(2 * e, 2)],
            send_sem=ss.at[to],
            recv_sem=rs.at[e],
            device_id=device(z, y, to // 2, to % 2),
            device_id_type=MESH,
        )

    def panel_step(k, carry):
        t = lax.rem(q + jnp.where(k == 0, 2, jnp.where(k == 1, 1, jnp.where(k == 2, 3, 0))), 4)
        cols = pl.ds(pl.multiple_of(t * 256, 256), 256)
        both = dot(hs[...], uhi[:, cols])
        part = both[:256] + both[256:] + dot(hs[:256, :], ulo[:, cols])
        for r in range(2):
            pq[2 * r + c, :, cols] = part[r * BS : r * BS + BS]
        for core in range(2):
            to = 2 * t + core
            turned = [part[r * BS : r * BS + BS, core * BS : core * BS + BS].T for r in range(2)]

            @pl.when(to == e)
            def _():
                for r in range(2):
                    ptl[2 * e + r] = turned[r]

            @pl.when(to != e)
            def _():
                for r in range(2):
                    st[to, r] = turned[r]
                piece(to).start()

        return carry

    lax.fori_loop(0, 4, panel_step, 0)
    for r in range(2):
        core_copy(pq, r, px_s, px_r).start()
    acc[...] = v_ref[...]

    def square_step(s, carry):
        k = s // 2
        t = lax.rem(q + jnp.where(k == 0, 0, jnp.where(k == 1, 1, jnp.where(k == 2, 3, 2))), 4)
        m = 2 * t + lax.rem(s + c, 2)

        @pl.when(m != e)
        def _():
            pltpu.make_async_remote_copy(
                src_ref=st.at[m],
                dst_ref=ptl.at[pl.ds(2 * m, 2)],
                send_sem=ss.at[m],
                recv_sem=rs.at[m],
                device_id=partner,
                device_id_type=MESH,
            ).wait_recv()

        hi, lo = halves(jnp.concatenate([ptl[2 * m], ptl[2 * m + 1]], 1))
        rows = pl.ds(pl.multiple_of(m * 256, 256), 256)
        both = dot(jnp.concatenate([hi, lo], 0), uhi[rows, :])
        acc[...] += both[:BS] + both[BS:] + dot(hi, ulo[rows, :])
        return carry

    lax.fori_loop(0, 8, square_step, 0)

    for r in range(2):
        core_arrived(hq, r, hx_s, hx_r).wait_recv()
        core_arrived(pq, r, px_s, px_r).wait_recv()

    if not last:
        mine = sel_ref[0, e]
        for m in range(8):
            block = sel_ref[1, m]
            out_ref[0, 2 * m] = acc[:, m * BS : m * BS + BS]
            out_ref[0, 2 * m + 1] = -ptl[block]
            out_ref[1, 2 * m] = -pq[mine, :, m * BS : m * BS + BS]
            out_ref[1, 2 * m + 1] = hq[mine, block]
    else:
        def rows_of(half):
            for p in range(2):
                quarter = 2 * half + p
                yield p * 768, acc[:, pl.ds(pl.multiple_of(quarter * 256, 256), 256)]
                for a in range(4):
                    yield p * 768 + 256 + a * BS, -ptl[2 * (2 * quarter + a % 2) + a // 2]

        for at, value in rows_of(1 - c):
            xin[1, :, at : at + value.shape[1]] = value
        cross = pltpu.make_async_remote_copy(
            src_ref=xin.at[1],
            dst_ref=xin.at[0],
            send_sem=xs_s,
            recv_sem=xs_r,
            device_id=partner,
            device_id_type=MESH,
        )
        cross.start()
        mine_at = pl.ds(pl.multiple_of(c * BS, BS), BS)
        for at, value in rows_of(c):
            out_ref[0, mine_at, at : at + value.shape[1]] = value
        for a in range(4):
            rows = slice(256 + a * BS, 256 + a * BS + BS)
            for p in range(2):
                quarter = 2 * c + p
                cols = pl.ds(pl.multiple_of(quarter * 256, 256), 256)
                out_ref[0, rows, p * 768 : p * 768 + 256] = -pq[a, :, cols]
                for b in range(4):
                    block = 2 * (2 * quarter + b % 2) + b // 2
                    to = p * 768 + 256 + b * BS
                    out_ref[0, rows, to : to + BS] = hq[a, block]
        cross.wait()
        out_ref[0, pl.ds(pl.multiple_of((1 - c) * BS, BS), BS), :] = xin[0]

    for r in range(2):
        core_copy(hq, r, hx_s, hx_r).wait_send()
        core_copy(pq, r, px_s, px_r).wait_send()

    def sent(to, carry):
        @pl.when(to != e)
        def _():
            piece(to).wait_send()

        return carry

    lax.fori_loop(0, 8, sent, 0)


def level(depth, sel, held, update, pivot):
    last = depth == 3
    shape = (1, 768, 1536) if last else (2, 16, BS, BS)
    sem = pltpu.SemaphoreType.DMA
    return pl.pallas_call(
        functools.partial(level_kernel, last),
        out_shape=jax.ShapeDtypeStruct(shape, F32),
        in_specs=[SMEM, VMEM, VMEM, VMEM],
        out_specs=VMEM,
        scratch_shapes=[
            pltpu.VMEM((4, 16, BS, BS), F32),
            pltpu.VMEM((4, BS, SEP), F32),
            pltpu.VMEM((ANC, SEP), BF16),
            pltpu.VMEM((ANC, SEP), BF16),
            pltpu.VMEM((512, ANC), BF16),
            pltpu.VMEM((8, 2, BS, BS), F32),
            pltpu.VMEM((16, BS, BS), F32),
            pltpu.VMEM((BS, SEP), F32),
            pltpu.VMEM((2, BS, 1536), F32),
            sem,
            sem,
            sem((8,)),
            sem((8,)),
            sem((2,)),
            sem((2,)),
            sem((2,)),
            sem((2,)),
        ],
        compiler_params=pltpu.CompilerParams(
            collective_id=1 + depth, has_side_effects=True, vmem_limit_bytes=56 * 2**20
        ),
        name="level_%d" % (depth + 1),
    )(sel, held, update, pivot)


def shards(
    root_inverse,
    blocks_one,
    blocks_two,
    blocks_three,
    blocks_four,
    update_one,
    update_two,
    update_three,
    update_four,
    pivot_one,
    pivot_two,
    pivot_three,
    pivot_four,
):
    z, y, _, c = place()
    leaf = z * 4 + y
    groups = (("zb", "ya", "yb"), ("ya", "yb"), ("yb",), ())
    updates = (update_one, update_two, update_three, update_four)
    pivots = (pivot_one, pivot_two, pivot_three, pivot_four)
    lists = (blocks_two, blocks_three, blocks_four, blocks_four)
    full, rows = [], []
    for axes, update, pivot in zip(groups, updates, pivots):
        value = lax.dynamic_slice_in_dim(pivot, c * BS, BS, 0)
        if axes:
            update = lax.all_gather(update, axes, axis=1, tiled=True)
            value = lax.all_gather(value, axes, axis=1, tiled=True)
        full.append(lax.all_gather(update, "col", axis=0, tiled=True))
        rows.append(value)
    held = spread(pick(blocks_one, root_inverse))
    for depth in range(4):
        ids = lax.dynamic_index_in_dim(
            lists[depth], leaf // max(1, 4 >> depth), 0, keepdims=False
        )
        listed = ids.reshape(4, 4)[:, 2:] - 6 * jnp.arange(4, dtype=jnp.int32)[:, None] - 2
        chosen = jnp.clip(listed.reshape(8), 0, 3)
        quarters = jnp.arange(8, dtype=jnp.int32) // 2
        sel = jnp.stack([chosen, 4 * quarters + 2 * (chosen % 2) + chosen // 2])
        held = level(depth, sel, held, full[depth], rows[depth])
    return held


def solution(mesh):
    mesh = Mesh(mesh.devices.reshape(2, 2, 2, 2, 4, 2), AXES)
    leaf = AXES[:4]
    placed = (
        P(leaf, ("row", "col")),
        P(),
        P(),
        P(),
        P(),
        P("col", leaf),
        P("col", leaf),
        P("col", leaf),
        P("col", leaf),
        P("row", leaf),
        P("row", leaf),
        P("row", leaf),
        P("row", leaf),
    )
    return jax.shard_map(
        shards, mesh=mesh, in_specs=placed, out_specs=P(leaf, "row", "col"), check_vma=False
    )
```

time: 1060 us -> 418 us (0.39); the launches traced: 1050 us -> 417 us
  waiting for transfers between devices: 473 us -> 178 us
  local copies, waits for them, and re-layouts: 260 us -> 12.4 us
  Pallas kernels: 0 us -> 165 us
  other arithmetic: 149 us -> 1.86 us
  blocking collectives: 87.1 us -> 46.1 us
  matrix products: 37.1 us -> 0 us
  starting transfers between devices: 27.7 us -> 0.23 us
    psum x9 -> x0, waiting for transfers between devices: 310 us -> none  [the longest x4 110 us: shards(): panel = lax.psum(part, 'col')]
    all_gather x0 -> x7, waiting for transfers between devices: none -> 176 us  [the longest x3 176 us: shards(): update = lax.all_gather(update, axes, axis=1, tiled=True)]
    pallas_call x0 -> x6, Pallas kernels: none -> 165 us  [the longest x4 112 us: level(): pl.pallas_call(functools.partial(level_kernel, last), out_shape=jax.Shape...]
    ppermute x12 -> x0, waiting for transfers between devices: 115 us -> none  [swapped(): return lax.ppermute(value, axis, pairs)]
    all_to_all x3 -> x0, blocking collectives: 87.1 us -> none  [shards(): lax.all_to_all(panel, 'row', split_axis=2, concat_axis=1, tiled=True)]
    gather x10 -> x0, local copies, waits for them, and re-layouts: 65.1 us -> none  [the longest x5 36.1 us: select_blocks(): picked = jnp.take(shaped, row_ids, axis=0)]
    select_n x21 -> x0, other arithmetic: 59 us -> none  [the longest x4 30.2 us: select_blocks(): picked = jnp.take(shaped, row_ids, axis=0)]
    concatenate x16 -> x0, other arithmetic: 54.6 us -> none  [the longest x4 43.7 us: assemble(): jnp.concatenate([top, bottom], 1)]
  transfers between devices with their start and end apart: 23 -> 7, of which waited for: 22 -> 3; matrix products, arithmetic and copies ran while one was open for 4% -> 1% of each run, Pallas kernels for 0% -> 33%
where the time goes in v1:
time: 418 us; the launch traced here: 417 us
  waiting for transfers between devices  178 us (43%)
  Pallas kernels  165 us (39%)
  blocking collectives  46.1 us (11%)
  between operations  13.7 us (3%)
  local copies, waits for them, and re-layouts  12.4 us (3%)
    all_gather x3, waiting for transfers between devices, shards(): update = lax.all_gather(update, axes, axis=1, tiled=True)  176 us
    pallas_call x4, Pallas kernels, level(): pl.pallas_call(functools.partial(level_kernel, last), out_shape=jax.Shape...  112 us
    pallas_call x1, Pallas kernels, spread(): pl.pallas_call(spread_kernel, out_shape=jax.ShapeDtypeStruct((2, 16, BS,...  48.5 us
    all_gather x3, blocking collectives, shards(): value = lax.all_gather(value, axes, axis=1, tiled=True)  46.1 us
    unnamed x17, local copies, waits for them, and re-layouts  9.58 us
  transfers between devices with their start and end apart: 7, of which 3 were waited for; matrix products, arithmetic and copies ran while one was open for 1% of the time, Pallas kernels for 33%

profile of v1, /device:TPU:1, one launch (start us, length us, event | category | flops | bytes accessed | tf_op | source)
XLA Modules:
  0.0 417.5 jit_solution(5036627003189257392)
XLA Ops:
  6.5 0.7 all-gather.8.cloned.1.call-update
  7.3 0.0 all-gather.12.cloned.1.call-start
  7.3 0.7 all-gather.12.cloned.1.call-update
  8.0 0.0 all-gather.16.cloned.1.call-start
  8.1 0.7 all-gather.16.cloned.1.call-update
  8.7 0.0 all-gather.10.cloned.1.call-start
  8.8 61.7 %all-gather.8.cloned.1.call-done = f32[1024,1024]{1,0:T(8,128)} async-done(((f32[1024,128]{1,0:T(8,128)}), f32[1024,1024]{1,0:T(8,128)}) %all-gather.8.cloned.1.call-update) | async-done | bytes 4194320 | tf_op jit(solution)/shard_map/all_gather | solution.py:452
  70.5 0.0 all-gather.10.cloned.1.call-update
  70.5 0.0 all-gather.14.cloned.1.call-start
  70.5 52.7 %all-gather.12.cloned.1.call-done = f32[1024,1024]{1,0:T(8,128)} async-done(((f32[1024,256]{1,0:T(8,128)}), f32[1024,1024]{1,0:T(8,128)}) %all-gather.12.cloned.1.call-update) | async-done | bytes 4194320 | tf_op jit(solution)/shard_map/all_gather | solution.py:452
  123.2 0.0 all-gather.14.cloned.1.call-update
  123.2 0.0 all-gather.18.cloned.1.call-start
  123.3 61.3 %all-gather.16.cloned.1.call-done = f32[1024,1024]{1,0:T(8,128)} async-done(((f32[1024,512]{1,0:T(8,128)}), f32[1024,1024]{1,0:T(8,128)}) %all-gather.16.cloned.1.call-update) | async-done | bytes 4194320 | tf_op jit(solution)/shard_map/all_gather | solution.py:452
  184.5 0.0 all-gather.18.cloned.1.call-update
  184.5 0.0 all-gather.20.cloned.1.call-start
  184.6 0.7 all-gather.20.cloned.1.call-update
  185.3 0.7 fusion.1
  186.1 0.1 reshape.331
  186.1 0.1 reshape.332
  186.2 0.7 fusion.3
  186.9 0.1 reshape.333
  187.0 0.1 add_clamp_fusion
  187.1 0.1 min.30
  187.2 3.4 copy-done.2
  190.6 4.7 %pick.1.m_ref = f32[2,4,4,128,128]{4,3,2,1,0:T(8,128)S(1)} custom-call(s32[2,16]{1,0:T(2,128)S(1)} %copy-done.4, f32[1024,2048]{1,0:T(8,128)S(1)} %copy-done.2), custom_call_target="tpu_custom_call" | custom-call | tf_op jit(solution)/shard_map/pick/pallas_call | solution.py:71
  195.3 0.0 copy-start.7
  195.3 0.0 copy-start.6
  195.3 0.0 copy-start.5
  195.3 48.5 %spread.1.h_ref = f32[2,16,128,128]{3,2,1,0:T(8,128)S(1)} custom-call(f32[2,4,4,128,128]{4,3,2,1,0:T(8,128)S(1)} %pick.1.m_ref), custom_call_target="tpu_custom_call" | custom-call | tf_op jit(solution)/shard_map/spread/pallas_call | solution.py:186
  243.8 0.0 copy-start.3
  243.9 1.3 copy-done.3
  245.2 0.1 min.28
  245.2 0.1 min.26
  245.3 0.6 pad_add_fusion.2.sel_ref
  246.0 0.6 pad_add_fusion.1.sel_ref
  246.5 0.6 pad_add_fusion.sel_ref
  247.2 0.9 constant_dynamic-slice_fusion.v_ref
  248.1 8.4 %all_gather.38.v_ref = f32[128,1024]{1,0:T(8,128)} all-gather(f32[128,512]{1,0:T(8,128)S(1)} %constant_dynamic-slice_fusion.1), channel_id=1, replica_groups=mesh['za'=2,'zb'=2,'ya'=2,'yb'=2,'row'=4,'col'=2] {'yb'}, dimensions={1}, use_global_device_ids=true | all-gather | bytes 786432 | tf_op jit(solution)/shard_map/all_gather | solution.py:453
  256.5 11.8 %all_gather.35.v_ref = f32[128,1024]{1,0:T(8,128)} all-gather(f32[128,256]{1,0:T(8,128)S(1)} %constant_dynamic-slice_fusion.2), channel_id=1, replica_groups=mesh['za'=2,'zb'=2,'ya'=2,'yb'=2,'row'=4,'col'=2] {'ya','yb'}, dimensions={1}, use_global_device_ids=true | all-gather | bytes 655360 | tf_op jit(solution)/shard_map/all_gather | solution.py:453
  268.3 25.8 %all_gather.32.v_ref = f32[128,1024]{1,0:T(8,128)} all-gather(f32[128,128]{1,0:T(8,128)S(1)} %constant_dynamic-slice_fusion.3), channel_id=1, replica_groups=mesh['za'=2,'zb'=2,'ya'=2,'yb'=2,'row'=4,'col'=2] {'zb','ya','yb'}, dimensions={1}, use_global_device_ids=true | all-gather | bytes 589824 | tf_op jit(solution)/shard_map/all_gather | solution.py:453
  294.1 33.7 %level_1.1.h_ref = f32[2,16,128,128]{3,2,1,0:T(8,128)} custom-call(s32[2,8]{1,0:T(2,128)} %pad_add_fusion.2.sel_ref, f32[2,16,128,128]{3,2,1,0:T(8,128)} %copy-done.3, f32[2048,1024]{1,0:T(8,128)} %all-gather.10.cloned.1.call-done.u_ref, f32[128,1024]{1,0:T(8,128)} %all_gather.32.v_ref), custom_call_target="tpu_custom_call" | custom-call | tf_op jit(solution)/shard_map/level_1/pallas_call | solution.py:396
  327.8 0.0 all-gather.14.cloned.1.call-done.u_ref
  327.9 25.1 %level_2.1.h_ref = f32[2,16,128,128]{3,2,1,0:T(8,128)} custom-call(s32[2,8]{1,0:T(2,128)} %pad_add_fusion.1.sel_ref, f32[2,16,128,128]{3,2,1,0:T(8,128)} %level_1.1.h_ref, f32[2048,1024]{1,0:T(8,128)} %all-gather.14.cloned.1.call-done.u_ref, f32[128,1024]{1,0:T(8,128)} %all_gather.35.v_ref), custom_call_target="tpu_custom_call" | custom-call | tf_op jit(solution)/shard_map/level_2/pallas_call | solution.py:396
  353.0 0.0 all-gather.18.cloned.1.call-done.u_ref
  353.1 24.9 %level_3.1.h_ref = f32[2,16,128,128]{3,2,1,0:T(8,128)} custom-call(s32[2,8]{1,0:T(2,128)} %pad_add_fusion.sel_ref, f32[2,16,128,128]{3,2,1,0:T(8,128)} %level_2.1.h_ref, f32[2048,1024]{1,0:T(8,128)} %all-gather.18.cloned.1.call-done.u_ref, f32[128,1024]{1,0:T(8,128)} %all_gather.38.v_ref), custom_call_target="tpu_custom_call" | custom-call | tf_op jit(solution)/shard_map/level_3/pallas_call | solution.py:396
  378.0 0.0 all-gather.20.cloned.1.call-done.u_ref
  378.0 27.8 %level_4.1 = f32[1,768,1536]{2,1,0:T(8,128)} custom-call(s32[2,8]{1,0:T(2,128)} %pad_add_fusion.sel_ref, f32[2,16,128,128]{3,2,1,0:T(8,128)} %level_3.1.h_ref, f32[2048,1024]{1,0:T(8,128)} %all-gather.20.cloned.1.call-done.u_ref, f32[128,1024]{1,0:T(8,128)} %constant_dynamic-slice_fusion.v_ref), custom_call_target="tpu_custom_call" | custom-call | tf_op jit(solution)/shard_map/level_4/pallas_call | solution.py:396
  405.8 4.8 %copy.15 = f32[1,768,1536]{2,1,0:T(8,128)} copy(f32[1,768,1536]{2,1,0:T(8,128)} %level_4.1) | data formatting | bytes 9437184
  (19 shorter events, 0.1 us)
Async XLA Ops:
  6.5 240.7 %copy-start = (f32[256,1024]{1,0:T(8,128)S(1)}, f32[256,1024]{1,0:T(8,128)}, u32[]{:S(2)}) copy-start(f32[256,1024]{1,0:T(8,128)} %param.25) | copy-start | bytes 3145732
  6.5 63.9 %all-gather.8.cloned.1.call-start = ((), (), s32[]{:S(2)}) async-start(), calls=%async_computation | async-start | bytes 4718592 | tf_op jit(solution)/shard_map/all_gather | solution.py:452
  7.3 115.9 %all-gather.12.cloned.1.call-start = ((), (), s32[]{:S(2)}) async-start(), calls=%async_computation.2 | async-start | bytes 5242880 | tf_op jit(solution)/shard_map/all_gather | solution.py:452
  8.0 176.5 %all-gather.16.cloned.1.call-start = ((), (), s32[]{:S(2)}) async-start(), calls=%async_computation.4 | async-start | bytes 6291456 | tf_op jit(solution)/shard_map/all_gather | solution.py:452
  8.7 285.4 %all-gather.10.cloned.1.call-start = ((), (), s32[]{:S(2)}) async-start(), calls=%async_computation.1 | async-start | bytes 12582912 | tf_op jit(solution)/shard_map/all_gather | solution.py:454
  70.5 257.4 %all-gather.14.cloned.1.call-start = ((), (), s32[]{:S(2)}) async-start(), calls=%async_computation.3 | async-start | bytes 12582912 | tf_op jit(solution)/shard_map/all_gather | solution.py:454
  123.2 229.8 %all-gather.18.cloned.1.call-start = ((), (), s32[]{:S(2)}) async-start(), calls=%async_computation.5 | async-start | bytes 12582912 | tf_op jit(solution)/shard_map/all_gather | solution.py:454
  184.5 2.7 copy-start.4
  184.5 193.4 %all-gather.20.cloned.1.call-start = ((), (), s32[]{:S(2)}) async-start(), calls=%async_computation.6 | async-start | bytes 12582912 | tf_op jit(solution)/shard_map/all_gather | solution.py:454
  187.2 3.4 copy-start.2
  195.3 51.8 %copy-start.7 = (f32[256,128]{1,0:T(8,128)S(1)}, f32[256,128]{1,0:T(8,128)}, u32[]{:S(2)}) copy-start(f32[256,128]{1,0:T(8,128)} %param.22) | copy-start | bytes 393220
  195.3 51.8 %copy-start.6 = (f32[256,256]{1,0:T(8,128)S(1)}, f32[256,256]{1,0:T(8,128)}, u32[]{:S(2)}) copy-start(f32[256,256]{1,0:T(8,128)} %param.23) | copy-start | bytes 786436
  195.3 51.8 %copy-start.5 = (f32[256,512]{1,0:T(8,128)S(1)}, f32[256,512]{1,0:T(8,128)}, u32[]{:S(2)}) copy-start(f32[256,512]{1,0:T(8,128)} %param.24) | copy-start | bytes 1572868
  243.8 1.3 copy-start.3
  378.0 32.6 %copy-start.1 = (f32[256,1024]{1,0:T(8,128)S(1)}, f32[256,1024]{1,0:T(8,128)}, u32[]{:S(2)}) copy-start(f32[256,1024]{1,0:T(8,128)} %param.25) | copy-start | bytes 3145732
Sparse Core Ops, SparseCore 0:
  8.9 61.4 all-gather.7
  72.1 51.0 all-gather.11
  124.9 59.6 all-gather.15
  186.0 23.9 all-gather.9
  211.5 23.9 all-gather.13
  237.0 23.8 all-gather.17
  262.6 23.8 all-gather.19

commit v2 on v0

v2 whole, which is shorter than its diff:
```python
import jax
import jax.numpy as jnp
from jax import lax
from jax.experimental import pallas as pl
from jax.experimental.pallas import tpu as pltpu
from jax.sharding import Mesh, PartitionSpec as P

SEP = 1024
ANC = 2048
BS = 128
UNIT = 256
AXES = ("za", "zb", "ya", "yb", "row", "col")
MESH = pl.DeviceIdType.MESH
F32 = jnp.float32
BF16 = jnp.bfloat16
SHARE = (4, 2, 2)


def place():
    z = lax.axis_index("za") * 2 + lax.axis_index("zb")
    y = lax.axis_index("ya") * 2 + lax.axis_index("yb")
    return z, y, lax.axis_index("row"), lax.axis_index("col")


def device(z, y, x, c):
    return (z // 2, z % 2, y // 2, y % 2, x, c)


def halves(value):
    high = value.astype(BF16)
    return high, (value - high.astype(F32)).astype(BF16)


def dot(a, b):
    return jnp.dot(a, b, preferred_element_type=F32)


def block_at(index, size):
    return pl.ds(pl.multiple_of(index * size, size), size)


def remote(src, dst, send, recv, to):
    return pltpu.make_async_remote_copy(
        src_ref=src, dst_ref=dst, send_sem=send, recv_sem=recv, device_id=to, device_id_type=MESH
    )


class Gather:
    def __init__(self, level, spot, u, v, ug, vg, sems):
        self.level, self.u, self.v, self.ug, self.vg = level, u, v, ug, vg
        self.z, self.y, self.x, self.c = spot
        self.own_sem, self.a_s, self.a_r, self.b_s, self.b_r, self.c_s, self.c_r, self.v_s, self.v_r = sems
        self.count = 8 >> level
        self.width = SEP // self.count
        self.share = SHARE[level]
        self.me = lax.rem(self.z * 4 + self.y, self.count)
        self.first = self.x if self.share == 4 else 2 * lax.rem(self.x, 2)
        self.units = 4 // self.share
        if self.share == 4:
            self.hops = ((1, 0, 1), (3, 0, 1), (2, 0, 1))
        else:
            self.hops = ((1, 0, 1), (3, 1, 1))

    def peer(self, d):
        base = (self.z * 4 + self.y) // self.count * self.count
        return lax.rem(self.me + d, self.count), base

    def leaf(self, member, base):
        at = base + member
        return device(at // 4, lax.rem(at, 4), self.x, self.c)

    def cols(self, member):
        return block_at(member, self.width)

    def rows(self, first, units):
        return pl.ds(pl.multiple_of(first * UNIT, UNIT), units * UNIT)

    def own(self):
        return (
            pltpu.make_async_copy(self.u, self.ug.at[self.c, :, self.cols(self.me)], self.own_sem.at[0]),
            pltpu.make_async_copy(
                self.v.at[block_at(self.c, BS), :], self.vg.at[:, self.cols(self.me)], self.own_sem.at[1]
            ),
        )

    def a_copy(self, d):
        member, base = self.peer(d)
        rows = self.rows(self.first, self.units)
        return remote(
            self.u.at[rows, :], self.ug.at[self.c, rows, self.cols(self.me)],
            self.a_s.at[d], self.a_r.at[self.me], self.leaf(member, base),
        )

    def v_copy(self, d):
        member, base = self.peer(d)
        return remote(
            self.v.at[block_at(self.c, BS), :], self.vg.at[:, self.cols(self.me)],
            self.v_s.at[d], self.v_r.at[self.me], self.leaf(member, base),
        )

    def a_arrived(self, member):
        rows = self.rows(self.first, self.units)
        there = self.ug.at[self.c, rows, self.cols(member)]
        return remote(there, there, self.a_s.at[0], self.a_r.at[member], device(self.z, self.y, self.x, 1 - self.c))

    def v_arrived(self, member):
        there = self.vg.at[:, self.cols(member)]
        return remote(there, there, self.v_s.at[0], self.v_r.at[member], device(self.z, self.y, self.x, 1 - self.c))

    def b_copy(self, n, member):
        step, first, units = self.hops[n]
        there = self.ug.at[self.c, self.rows(self.first + first, units), self.cols(member)]
        to = device(self.z, self.y, lax.rem(self.x + step, 4), self.c)
        return remote(there, there, self.b_s.at[n, member], self.b_r.at[n, member], to)

    def b_arrived(self, n, member):
        step, first, units = self.hops[n]
        source = lax.rem(self.x + 4 - step, 4)
        start = source if self.share == 4 else 2 * lax.rem(source, 2)
        there = self.ug.at[self.c, self.rows(start + first, units), self.cols(member)]
        return remote(
            there, there, self.b_s.at[n, member], self.b_r.at[n, member],
            device(self.z, self.y, self.x, 1 - self.c),
        )

    def c_copy(self, unit, half):
        there = self.ug.at[half, self.rows(unit, 1), :]
        return remote(
            there, there, self.c_s.at[unit], self.c_r.at[unit], device(self.z, self.y, self.x, 1 - self.c)
        )

    def unit(self, n):
        return lax.rem(self.first + n, 4)

    def begin(self):
        for copy in self.own():
            copy.start()

    def send(self):
        for d in range(1, self.count):
            self.a_copy(d).start()
            self.v_copy(d).start()

    def share_out(self):
        for copy in self.own():
            copy.wait()

        def step(d, carry):
            member = lax.rem(self.me + self.count - d, self.count)
            self.a_arrived(member).wait_recv()
            for n in range(len(self.hops)):
                self.b_copy(n, member).start()
            return carry

        lax.fori_loop(1, self.count, step, 0)
        for n in range(self.units):
            self.c_copy(self.unit(n), self.c).start()

    def collect(self):
        def step(d, carry):
            member = lax.rem(self.me + self.count - d, self.count)
            for n in range(len(self.hops)):
                self.b_arrived(n, member).wait_recv()
            self.v_arrived(member).wait_recv()
            return carry

        lax.fori_loop(1, self.count, step, 0)
        for n in range(self.units, 4):
            self.c_copy(self.unit(n), self.c).start()

    def wait_other(self, unit):
        self.c_copy(unit, 1 - self.c).wait_recv()

    def finish(self):
        def step(d, carry):
            self.a_copy(d).wait_send()
            self.v_copy(d).wait_send()
            member = lax.rem(self.me + self.count - d, self.count)
            for n in range(len(self.hops)):
                self.b_copy(n, member).wait_send()
            return carry

        lax.fori_loop(1, self.count, step, 0)
        for unit in range(4):
            self.c_copy(unit, self.c).wait_send()


def whole_kernel(
    tab_ref, mask_ref, sel_ref, root_ref, u1, u2, u3, u4, v1, v2, v3, v4,
    out_ref, ug1, ug2, ug3, ug4,
    rootv, picked, core_in, mine, y_in, ready, held, hq0, hq1, pq0, pq1, ptl0, ptl1, uhi, ulo, stage, hs, st, vg, acc, xin,
    root_sem, core_s, core_r, ys, yr, h_s, h_r,
    own1, a1s, a1r, b1s, b1r, c1s, c1r, w1s, w1r,
    own2, a2s, a2r, b2s, b2r, c2s, c2r, w2s, w2r,
    own3, a3s, a3r, b3s, b3r, c3s, c3r, w3s, w3r,
    c4s, c4r, v4_sem, stage_sem, ps, pr, hx_s, hx_r, px_s, px_r, xs_s, xs_r,
):
    spot = place()
    z, y, q, c = spot
    e = 2 * q + c
    partner = device(z, y, q, 1 - c)
    g1 = Gather(0, spot, u1, v1, ug1, vg.at[0], (own1, a1s, a1r, b1s, b1r, c1s, c1r, w1s, w1r))
    g2 = Gather(1, spot, u2, v2, ug2, vg.at[1], (own2, a2s, a2r, b2s, b2r, c2s, c2r, w2s, w2r))
    g3 = Gather(2, spot, u3, v3, ug3, vg.at[2], (own3, a3s, a3r, b3s, b3r, c3s, c3r, w3s, w3r))
    gathers = (g1, g2, g3)

    barrier = pltpu.get_barrier_semaphore()

    def signal(dev):
        pl.semaphore_signal(barrier, inc=1, device_id=dev, device_id_type=MESH)

    mine_f = z // 2

    def root_copy(j):
        return pltpu.make_async_copy(
            root_ref.at[:, :, j * BS : j * BS + BS], rootv.at[j], root_sem.at[j]
        )

    for j in range(16):
        root_copy(j).start()
    for g in gathers:
        g.begin()
    for t in range(8):

        @pl.when(t != e)
        def _():
            signal(device(z, y, t // 2, t % 2))

    for d in range(1, 8):
        member, base = g1.peer(d)
        signal(g1.leaf(member, base))
    for p in range(4):
        for r in range(2):
            j = 2 * r + c

            @pl.when(jnp.logical_not((p == z) & (j == y) & (mine_f == c)))
            def _():
                signal(device(p, j, q, mine_f))

    own = (mine_f == c) & (y % 2 == c)
    pl.semaphore_wait(barrier, jnp.where(own, 21, 22))

    g1.send()

    def u4_push(unit):
        rows = pl.ds(unit * UNIT, UNIT)
        return remote(u4.at[rows, :], ug4.at[rows, :], c4s.at[unit], c4r.at[unit], partner)

    def v4_copy():
        return pltpu.make_async_copy(v4.at[block_at(c, BS), :], acc.at[1], v4_sem)

    for unit in range(4):
        u4_push(unit).start()
    v4_copy().start()

    for j in range(16):
        root_copy(j).wait()

    def pick(n, carry):
        f, j = n // 4, n % 4
        for i in range(4):
            at = n * 4 + i
            block = rootv[tab_ref[32 + at], tab_ref[at]]
            picked[f, j, i % 2 * 2 + i // 2] = (block * mask_ref[at]).T
        return carry

    lax.fori_loop(0, 8, pick, 0)
    core = remote(picked.at[1 - c], core_in, core_s, core_r, partner)
    core.start()
    core.wait()
    mine[...] = picked[c] + core_in[...]

    def y_copy(d):
        to = lax.rem(y + d, 4)
        return remote(mine.at[to], y_in.at[d - 1], ys.at[d - 1], yr.at[d - 1], device(z, to, q, c))

    for d in (2, 1, 3):
        y_copy(d).start()
    for d in (1, 3, 2):
        y_copy(d).wait()
    ready[...] = mine[y] + y_in[0] + y_in[1] + y_in[2]

    def h_copy(k, d):
        return remote(
            ready, held.at[y // 2, pl.ds(4 * z, 4)], h_s.at[k * 4 + d], h_r.at[z * 2 + y // 2],
            device(2 * c + k, lax.rem(y + d, 4), q, y % 2),
        )

    def to_self(k):
        return (2 * c + k == z) & (y % 2 == c)

    for d in (2, 1, 3):
        for k in range(2):
            h_copy(k, d).start()
    for k in range(2):

        @pl.when(jnp.logical_not(to_self(k)))
        def _():
            h_copy(k, 0).start()

        @pl.when(to_self(k))
        def _():
            held[y // 2, pl.ds(4 * z, 4)] = ready[...]

    g1.share_out()
    for p in range(4):
        for r in range(2):

            @pl.when(jnp.logical_not((p == z) & (2 * r + c == y) & (mine_f == c)))
            def _():
                there = held.at[r, pl.ds(4 * p, 4)]
                remote(there, there, h_s.at[0], h_r.at[p * 2 + r], partner).wait_recv()

    g2.send()
    for d in (2, 1, 3):
        for k in range(2):
            h_copy(k, d).wait_send()
    for k in range(2):

        @pl.when(jnp.logical_not(to_self(k)))
        def _():
            h_copy(k, 0).wait_send()

    def pair_copy(ref, at, r, s_sem, r_sem):
        return remote(
            ref.at[2 * r + c], ref.at[2 * r + c], s_sem.at[at, r], r_sem.at[at, r], partner
        )

    def pair_arrived(ref, at, r, s_sem, r_sem):
        there = ref.at[2 * r + 1 - c]
        return remote(there, there, s_sem.at[at, r], r_sem.at[at, r], partner)

    def split_update(depth):
        def unit_of(n):
            first = gathers[depth].first if depth < 3 else 0
            return lax.rem(first + n // 2, 4), lax.rem(n + c, 2)

        def fetch(n, slot):
            unit, half = unit_of(n)
            rows = pl.ds(pl.multiple_of(unit * UNIT, UNIT), UNIT)
            if depth < 3:
                pltpu.make_async_copy(
                    gathers[depth].ug.at[half, rows, :], stage.at[slot], stage_sem.at[slot]
                ).start()
            else:

                @pl.when(half == c)
                def _():
                    pltpu.make_async_copy(u4.at[rows, :], stage.at[slot], stage_sem.at[slot]).start()

                @pl.when(half != c)
                def _():
                    pltpu.make_async_copy(ug4.at[rows, :], stage.at[slot], stage_sem.at[slot]).start()

        def arrived(n):
            unit, half = unit_of(n)

            @pl.when(half != c)
            def _():
                if depth < 3:
                    gathers[depth].wait_other(unit)
                else:
                    rows = pl.ds(pl.multiple_of(unit * UNIT, UNIT), UNIT)
                    remote(
                        ug4.at[rows, :], ug4.at[rows, :], c4s.at[unit], c4r.at[unit], partner
                    ).wait_recv()

        def step(n, carry):
            slot = lax.rem(n, 2)

            @pl.when(n + 1 < 8)
            def _():
                arrived(n + 1)
                fetch(n + 1, 1 - slot)

            pltpu.make_async_copy(
                u4.at[pl.ds(0, UNIT), :], stage.at[slot], stage_sem.at[slot]
            ).wait()
            unit, half = unit_of(n)
            for i in range(2):
                block = half * 8 + unit * 2 + i
                quarter, j = block // 4, lax.rem(block, 4)
                to = (2 * quarter + lax.rem(j, 2)) * 2 + j // 2
                hi, lo = halves(stage[slot, i * BS : i * BS + BS, :])
                uhi[block_at(to, BS), :] = hi
                ulo[block_at(to, BS), :] = lo
            return carry

        arrived(0)
        fetch(0, 0)
        lax.fori_loop(0, 8, step, 0)

    def level(depth):
        last = depth == 3
        at = depth % 2
        hq, pq, ptl = ((hq0, pq0, ptl0), (hq1, pq1, ptl1))[at]
        for r in range(2):
            for b in range(16):
                value = held[r, b]
                hi, lo = halves(value)
                hs[r * BS : r * BS + BS, b * BS : b * BS + BS] = hi
                hs[256 + r * BS : 256 + r * BS + BS, b * BS : b * BS + BS] = lo
                hq[2 * r + c, b] = value
            pair_copy(hq, at, r, hx_s, hx_r).start()
        if not last:
            gathers[depth].collect()
        split_update(depth)

        def piece(to):
            return remote(
                st.at[to], ptl.at[pl.ds(2 * e, 2)], ps.at[to], pr.at[at, e],
                device(z, y, to // 2, lax.rem(to, 2)),
            )

        def panel_step(k, carry):
            step = jnp.where(k == 0, 2, jnp.where(k == 1, 1, jnp.where(k == 2, 3, 0)))
            t = lax.rem(q + step, 4)
            cols = block_at(t, 256)
            both = dot(hs[...], uhi[:, cols])
            part = both[:256] + both[256:] + dot(hs[:256, :], ulo[:, cols])
            for r in range(2):
                pq[2 * r + c, :, cols] = part[r * BS : r * BS + BS]
            for core in range(2):
                to = 2 * t + core
                turned = [
                    part[r * BS : r * BS + BS, core * BS : core * BS + BS].T for r in range(2)
                ]

                @pl.when(to == e)
                def _():
                    for r in range(2):
                        ptl[2 * e + r] = turned[r]

                @pl.when(to != e)
                def _():
                    for r in range(2):
                        st[to, r] = turned[r]
                    piece(to).start()

            return carry

        lax.fori_loop(0, 4, panel_step, 0)
        for r in range(2):
            pair_copy(pq, at, r, px_s, px_r).start()
        if last:
            v4_copy().wait()
            acc[0] = acc[1]
        else:
            acc[0] = vg[depth]

        def square_step(s, carry):
            k = s // 2
            step = jnp.where(k == 0, 0, jnp.where(k == 1, 1, jnp.where(k == 2, 3, 2)))
            m = 2 * lax.rem(q + step, 4) + lax.rem(s + c, 2)

            @pl.when(m != e)
            def _():
                there = ptl.at[pl.ds(2 * m, 2)]
                remote(there, there, ps.at[m], pr.at[at, m], partner).wait_recv()

            hi, lo = halves(jnp.concatenate([ptl[2 * m], ptl[2 * m + 1]], 1))
            rows = block_at(m, 256)
            both = dot(jnp.concatenate([hi, lo], 0), uhi[rows, :])
            acc[0] += both[:BS] + both[BS:] + dot(hi, ulo[rows, :])
            return carry

        lax.fori_loop(0, 8, square_step, 0)
        for r in range(2):
            pair_arrived(hq, at, r, hx_s, hx_r).wait_recv()
            pair_arrived(pq, at, r, px_s, px_r).wait_recv()

        if not last:
            chosen = sel_ref[16 * depth + e]
            for m in range(8):
                block = sel_ref[16 * depth + 8 + m]
                held[0, 2 * m] = acc[0, :, m * BS : m * BS + BS]
                held[0, 2 * m + 1] = -ptl[block]
                held[1, 2 * m] = -pq[chosen, :, m * BS : m * BS + BS]
                held[1, 2 * m + 1] = hq[chosen, block]
        else:

            def rows_of(half):
                for p in range(2):
                    quarter = 2 * half + p
                    yield p * 768, acc[0, :, block_at(quarter, 256)]
                    for a in range(4):
                        yield p * 768 + 256 + a * BS, -ptl[2 * (2 * quarter + a % 2) + a // 2]

            for to, value in rows_of(1 - c):
                xin[1, :, to : to + value.shape[1]] = value
            cross = remote(xin.at[1], xin.at[0], xs_s, xs_r, partner)
            cross.start()
            for to, value in rows_of(c):
                out_ref[0, block_at(c, BS), to : to + value.shape[1]] = value
            for a in range(4):
                rows = slice(256 + a * BS, 256 + a * BS + BS)
                for p in range(2):
                    quarter = 2 * c + p
                    out_ref[0, rows, p * 768 : p * 768 + 256] = -pq[a, :, block_at(quarter, 256)]
                    for b in range(4):
                        block = 2 * (2 * quarter + b % 2) + b // 2
                        to = p * 768 + 256 + b * BS
                        out_ref[0, rows, to : to + BS] = hq[a, block]
            cross.wait()
            out_ref[0, block_at(1 - c, BS), :] = xin[0]

        for r in range(2):
            pair_copy(hq, at, r, hx_s, hx_r).wait_send()
            pair_copy(pq, at, r, px_s, px_r).wait_send()

        def sent(to, carry):
            @pl.when(to != e)
            def _():
                piece(to).wait_send()

            return carry

        lax.fori_loop(0, 8, sent, 0)

    level(0)
    g2.share_out()
    g3.send()
    level(1)
    g3.share_out()
    level(2)
    level(3)
    for g in gathers:
        g.finish()
    for unit in range(4):
        u4_push(unit).wait_send()


def whole(tab, mask, sel, root, updates, pivots):
    dma = pltpu.SemaphoreType.DMA
    any_space = pl.BlockSpec(memory_space=pl.ANY)
    smem = pl.BlockSpec(memory_space=pltpu.SMEM)
    gather_sems = []
    for depth in range(3):
        n = 8 >> depth
        gather_sems += [
            dma((2,)), dma((n,)), dma((n,)), dma((3, n)), dma((3, n)), dma((4,)), dma((4,)), dma((n,)), dma((n,)),
        ]
    outs = pl.pallas_call(
        whole_kernel,
        out_shape=[jax.ShapeDtypeStruct((1, 768, 1536), F32)]
        + [jax.ShapeDtypeStruct((2, 1024, 1024), F32)] * 3
        + [jax.ShapeDtypeStruct((1024, 1024), F32)],
        in_specs=[smem] * 3 + [any_space] * 9,
        out_specs=[pl.BlockSpec(memory_space=pltpu.VMEM)] + [any_space] * 4,
        scratch_shapes=[
            pltpu.VMEM((16, 8, BS, BS), F32),
            pltpu.VMEM((2, 4, 4, BS, BS), F32),
            pltpu.VMEM((4, 4, BS, BS), F32),
            pltpu.VMEM((4, 4, BS, BS), F32),
            pltpu.VMEM((3, 4, BS, BS), F32),
            pltpu.VMEM((4, BS, BS), F32),
            pltpu.VMEM((2, 16, BS, BS), F32),
            pltpu.VMEM((4, 16, BS, BS), F32),
            pltpu.VMEM((4, 16, BS, BS), F32),
            pltpu.VMEM((4, BS, SEP), F32),
            pltpu.VMEM((4, BS, SEP), F32),
            pltpu.VMEM((16, BS, BS), F32),
            pltpu.VMEM((16, BS, BS), F32),
            pltpu.VMEM((ANC, SEP), BF16),
            pltpu.VMEM((ANC, SEP), BF16),
            pltpu.VMEM((2, UNIT, SEP), F32),
            pltpu.VMEM((512, ANC), BF16),
            pltpu.VMEM((8, 2, BS, BS), F32),
            pltpu.VMEM((3, BS, SEP), F32),
            pltpu.VMEM((2, BS, SEP), F32),
            pltpu.VMEM((2, BS, 1536), F32),
            dma((16,)),
            dma,
            dma,
            dma((3,)),
            dma((3,)),
            dma((8,)),
            dma((8,)),
        ]
        + gather_sems
        + [
            dma((4,)),
            dma((4,)),
            dma,
            dma((2,)),
            dma((8,)),
            dma((2, 8)),
            dma((2, 2)),
            dma((2, 2)),
            dma((2, 2)),
            dma((2, 2)),
            dma,
            dma,
        ],
        compiler_params=pltpu.CompilerParams(
            collective_id=0, has_side_effects=True, vmem_limit_bytes=60 * 2**20
        ),
        name="whole",
    )(tab, mask, sel, root, *updates, *pivots)
    return outs[0]


def shards(
    root_inverse,
    blocks_one,
    blocks_two,
    blocks_three,
    blocks_four,
    update_one,
    update_two,
    update_three,
    update_four,
    pivot_one,
    pivot_two,
    pivot_three,
    pivot_four,
):
    z, y, x, c = place()
    leaf = z * 4 + y
    rows = lax.dynamic_slice_in_dim(blocks_one, z * 4, 4, 1)[:, None, :] - leaf * 8
    cols = lax.dynamic_slice_in_dim(blocks_one, x * 4, 4, 1)[:, :, None] - (x * 2 + c) * 16
    rows, cols = jnp.broadcast_arrays(rows, cols)
    valid = (rows >= 0) & (rows < 8) & (cols >= 0) & (cols < 16)
    tab = jnp.concatenate([jnp.clip(rows, 0, 7).reshape(32), jnp.clip(cols, 0, 15).reshape(32)])
    mask = valid.reshape(32).astype(F32)
    quarters = jnp.arange(8, dtype=jnp.int32) // 2
    sel = []
    for depth, lists in enumerate((blocks_two, blocks_three, blocks_four)):
        ids = lax.dynamic_index_in_dim(lists, leaf // (4 >> depth), 0, keepdims=False)
        chosen = jnp.clip(ids.reshape(4, 4)[:, 2:].reshape(8) - 6 * quarters - 2, 0, 3)
        sel += [chosen, 4 * quarters + 2 * (chosen % 2) + chosen // 2]
    return whole(
        tab,
        mask,
        jnp.concatenate(sel),
        root_inverse.reshape(8, BS, 2048),
        (update_one, update_two, update_three, update_four),
        (pivot_one, pivot_two, pivot_three, pivot_four),
    )


def solution(mesh):
    mesh = Mesh(mesh.devices.reshape(2, 2, 2, 2, 4, 2), AXES)
    leaf = AXES[:4]
    placed = (
        P(leaf, ("row", "col")),
        P(),
        P(),
        P(),
        P(),
        P("col", leaf),
        P("col", leaf),
        P("col", leaf),
        P("col", leaf),
        P("row", leaf),
        P("row", leaf),
        P("row", leaf),
        P("row", leaf),
    )
    return jax.shard_map(
        shards, mesh=mesh, in_specs=placed, out_specs=P(leaf, "row", "col"), check_vma=False
    )
```

time: 1060 us -> 223 us (0.21); the launches traced: 1050 us -> 222 us
  waiting for transfers between devices: 473 us -> 0 us
  local copies, waits for them, and re-layouts: 260 us -> 8.55 us
  Pallas kernels: 0 us -> 211 us
  other arithmetic: 149 us -> 2.41 us
  blocking collectives: 87.1 us -> 0 us
  matrix products: 37.1 us -> 0 us
  starting transfers between devices: 27.7 us -> 0 us
  between operations: 14.2 us -> 0.03 us
    psum x9 -> x0, waiting for transfers between devices: 310 us -> none  [the longest x4 110 us: shards(): panel = lax.psum(part, 'col')]
    pallas_call x0 -> x1, Pallas kernels: none -> 211 us  [whole(): pl.pallas_call(whole_kernel, out_shape=[jax.ShapeDtypeStruct((1, 768, 153...]
    ppermute x12 -> x0, waiting for transfers between devices: 115 us -> none  [swapped(): return lax.ppermute(value, axis, pairs)]
    all_to_all x3 -> x0, blocking collectives: 87.1 us -> none  [shards(): lax.all_to_all(panel, 'row', split_axis=2, concat_axis=1, tiled=True)]
    gather x10 -> x0, local copies, waits for them, and re-layouts: 65.1 us -> none  [the longest x5 36.1 us: select_blocks(): picked = jnp.take(shaped, row_ids, axis=0)]
    select_n x21 -> x0, other arithmetic: 59 us -> none  [the longest x4 30.2 us: select_blocks(): picked = jnp.take(shaped, row_ids, axis=0)]
    concatenate x16 -> x1, other arithmetic: 54.6 us -> 0.6 us  [shards(): jnp.concatenate([jnp.clip(rows, 0, 7).reshape(32), jnp.clip(cols, 0, 15)....]
    another operation x9 -> x0, local copies, waits for them, and re-layouts: 51.1 us -> none  [the longest x6 40.9 us: select_blocks(): shaped = tile.reshape(rows // block, block, cols // block, block)]
  transfers between devices with their start and end apart: 23 -> 0, of which waited for: 22 -> 0; matrix products, arithmetic and copies ran while one was open for 4% -> 0% of each run, Pallas kernels for 0% -> 0%
where the time goes in v2:
time: 223 us; the launch traced here: 222 us
  Pallas kernels  211 us (95%)
  local copies, waits for them, and re-layouts  8.55 us (4%)
  other arithmetic  2.41 us (1%)
    pallas_call x1, Pallas kernels, whole(): pl.pallas_call(whole_kernel, out_shape=[jax.ShapeDtypeStruct((1, 768, 153...  211 us
    unnamed x3, local copies, waits for them, and re-layouts  5.54 us

profile of v2, /device:TPU:1, one launch (start us, length us, event | category | flops | bytes accessed | tf_op | source)
XLA Modules:
  0.0 222.3 jit_solution(14407181981232320101)
XLA Ops:
  0.0 0.0 copy-start
  0.0 0.7 copy-done
  0.7 0.7 fusion.2
  1.4 0.1 reshape.44
  1.5 0.1 slice.9
  1.6 0.1 reshape.45
  1.7 0.1 reshape.48
  1.8 0.1 slice.11
  1.9 0.1 reshape.49
  2.0 0.8 compare_and_fusion
  2.8 0.8 broadcast_clamp_fusion.1
  3.7 0.1 reshape.46
  3.7 0.1 slice.10
  3.8 0.1 reshape.47
  3.9 0.6 concatenate.7.sel_ref
  4.5 0.1 and_convert_fusion
  4.6 0.7 reshape.51.mask_ref
  5.3 0.1 min.42
  5.4 0.1 broadcast_in_dim.19
  5.5 0.1 min.45
  5.5 0.6 pad_add_fusion.tab_ref
  6.1 211.3 %whole.1 = (f32[1,768,1536]{2,1,0:T(8,128)}, f32[2,1024,1024]{2,1,0:T(8,128)}, f32[2,1024,1024]{2,1,0:T(8,128)}, f32[2,1024,1024]{2,1,0:T(8,128)}, f32[1024,1024]{1,0:T(8,128)}) custom-call(s32[64]{0:T(128)} %pad_add_fusion.tab_ref, f32[32]{0:T(128)} %reshape.51.mask_ref, s32[48]{0:T(128)} %concatenate.7.sel_ref, f32[8,128,2048]{2,1,0:T(8,128)} %bitcast.1, ...), custom_call_target="tpu_custom_call" | custom-call | tf_op jit(solution)/shard_map/whole/pallas_call | solution.py:543
  217.5 4.8 %copy.15 = f32[1,768,1536]{2,1,0:T(8,128)} copy(f32[1,768,1536]{2,1,0:T(8,128)} %get-tuple-element.6) | data formatting | bytes 9437184
  (5 shorter events, 0.1 us)
Async XLA Ops:
  0.0 0.7 copy-start

commit v3 on v2

v3 whole, which is shorter than its diff:
```python
import jax
import jax.numpy as jnp
from jax import lax
from jax.experimental import pallas as pl
from jax.experimental.pallas import tpu as pltpu
from jax.sharding import Mesh, PartitionSpec as P

SEP = 1024
ANC = 2048
BS = 128
UNIT = 256
AXES = ("za", "zb", "ya", "yb", "row", "col")
MESH = pl.DeviceIdType.MESH
F32 = jnp.float32
BF16 = jnp.bfloat16


def place():
    z = lax.axis_index("za") * 2 + lax.axis_index("zb")
    y = lax.axis_index("ya") * 2 + lax.axis_index("yb")
    return z, y, lax.axis_index("row"), lax.axis_index("col")


def device(z, y, x, c):
    return (z // 2, z % 2, y // 2, y % 2, x, c)


def halves(value):
    high = value.astype(BF16)
    return high, (value - high.astype(F32)).astype(BF16)


def dot(a, b):
    return jnp.dot(a, b, preferred_element_type=F32)


def block_at(index, size):
    return pl.ds(pl.multiple_of(index * size, size), size)


def remote(src, dst, send, recv, to):
    return pltpu.make_async_remote_copy(
        src_ref=src, dst_ref=dst, send_sem=send, recv_sem=recv, device_id=to, device_id_type=MESH
    )


class Gather:
    def __init__(self, level, spot, u, v, ug, vg, sems):
        self.level, self.u, self.v, self.ug, self.vg = level, u, v, ug, vg
        self.z, self.y, self.x, self.c = spot
        self.own_sem, self.a_s, self.a_r, self.b_s, self.b_r, self.c_s, self.c_r, self.v_s, self.v_r = sems
        self.count = 8 >> level
        self.width = SEP // self.count
        self.me = lax.rem(self.z * 4 + self.y, self.count)
        self.first = self.x
        self.units = 1

    def peer(self, d):
        base = (self.z * 4 + self.y) // self.count * self.count
        return lax.rem(self.me + d, self.count), base

    def leaf(self, member, base):
        at = base + member
        return device(at // 4, lax.rem(at, 4), self.x, self.c)

    def cols(self, member):
        return block_at(member, self.width)

    def rows(self, first, units):
        return pl.ds(pl.multiple_of(first * UNIT, UNIT), units * UNIT)

    def own(self):
        return (
            pltpu.make_async_copy(self.u, self.ug.at[self.c, :, self.cols(self.me)], self.own_sem.at[0]),
            pltpu.make_async_copy(
                self.v.at[block_at(self.c, BS), :], self.vg.at[:, self.cols(self.me)], self.own_sem.at[1]
            ),
        )

    def a_copy(self, d):
        member, base = self.peer(d)
        rows = self.rows(self.first, self.units)
        return remote(
            self.u.at[rows, :], self.ug.at[self.c, rows, self.cols(self.me)],
            self.a_s.at[d], self.a_r.at[self.me], self.leaf(member, base),
        )

    def v_copy(self, d):
        member, base = self.peer(d)
        return remote(
            self.v.at[block_at(self.c, BS), :], self.vg.at[:, self.cols(self.me)],
            self.v_s.at[d], self.v_r.at[self.me], self.leaf(member, base),
        )

    def a_arrived(self, member):
        rows = self.rows(self.first, self.units)
        there = self.ug.at[self.c, rows, self.cols(member)]
        return remote(there, there, self.a_s.at[0], self.a_r.at[member], device(self.z, self.y, self.x, 1 - self.c))

    def v_arrived(self, member):
        there = self.vg.at[:, self.cols(member)]
        return remote(there, there, self.v_s.at[0], self.v_r.at[member], device(self.z, self.y, self.x, 1 - self.c))

    def b_place(self, n, member, source):
        if n < 2:
            rows = self.rows(source, 1)
        else:
            unit = lax.rem(source + (3, 1)[n - 2], 4)
            rows = pl.ds(pl.multiple_of(unit * UNIT + (n - 2) * BS, BS), BS)
        return self.ug.at[self.c, rows, self.cols(member)]

    def b_copy(self, n, member):
        there = self.b_place(n, member, self.x)
        to = device(self.z, self.y, lax.rem(self.x + (1, 3)[n % 2], 4), self.c)
        return remote(there, there, self.b_s.at[n, member], self.b_r.at[n, member], to)

    def b_arrived(self, n, member):
        there = self.b_place(n, member, lax.rem(self.x + (3, 1)[n % 2], 4))
        return remote(
            there, there, self.b_s.at[n, member], self.b_r.at[n, member],
            device(self.z, self.y, self.x, 1 - self.c),
        )

    def c_copy(self, unit, half):
        there = self.ug.at[half, self.rows(unit, 1), :]
        return remote(
            there, there, self.c_s.at[unit], self.c_r.at[unit], device(self.z, self.y, self.x, 1 - self.c)
        )

    def begin(self):
        for copy in self.own():
            copy.start()

    def send(self):
        for d in range(1, self.count):
            self.a_copy(d).start()

    def send_pivot(self):
        for d in range(1, self.count):
            self.v_copy(d).start()

    def others(self, body):
        def step(d, carry):
            body(lax.rem(self.me + self.count - d, self.count))
            return carry

        lax.fori_loop(1, self.count, step, 0)

    def share_out(self):
        for copy in self.own():
            copy.wait()

        def body(member):
            self.a_arrived(member).wait_recv()
            for n in range(2):
                self.b_copy(n, member).start()

        self.others(body)
        self.c_copy(self.x, self.c).start()

    def forward(self):
        def body(member):
            for n in range(2):
                self.b_arrived(n, member).wait_recv()
                self.b_copy(2 + n, member).start()

        self.others(body)
        for step in (3, 1):
            self.c_copy(lax.rem(self.x + step, 4), self.c).start()

    def collect(self):
        def body(member):
            for n in range(2, 4):
                self.b_arrived(n, member).wait_recv()

        self.others(body)
        self.c_copy(lax.rem(self.x + 2, 4), self.c).start()

    def collect_pivot(self):
        def step(d, carry):
            self.v_arrived(lax.rem(self.me + self.count - d, self.count)).wait_recv()
            return carry

        lax.fori_loop(1, self.count, step, 0)

    def wait_other(self, unit):
        self.c_copy(unit, 1 - self.c).wait_recv()

    def finish(self):
        def step(d, carry):
            self.a_copy(d).wait_send()
            self.v_copy(d).wait_send()
            return carry

        lax.fori_loop(1, self.count, step, 0)

        def body(member):
            for n in range(4):
                self.b_copy(n, member).wait_send()

        self.others(body)
        for unit in range(4):
            self.c_copy(unit, self.c).wait_send()


def whole_kernel(
    one_ref, two_ref, three_ref, four_ref, root_ref, u1, u2, u3, u4, v1, v2, v3, v4,
    out_ref, ug1, ug3, ug4,
    core_in, mine, y_in, ready, held, hq0, hq1, pq0, pq1, ptl0, ptl1,
    u2v, u2hi, u2lo, uhi0, ulo0, stage, hs, st, vg, acc, sq, xin,
    root_sem, core_s, core_r, ys, yr, h_s, h_r,
    own1, a1s, a1r, b1s, b1r, c1s, c1r, w1s, w1r,
    own3, a3s, a3r, b3s, b3r, c3s, c3r, w3s, w3r,
    c4s, c4r, v4_sem, u2_own, u2_s, u2_r, ag_s, ag_r, sg_s, sg_r,
    stage_sem, ps, pr, psr, prr, hx_s, hx_r, px_s, px_r, xs_s, xs_r,
):
    spot = place()
    z, y, q, c = spot
    e = 2 * q + c
    partner = device(z, y, q, 1 - c)
    g1 = Gather(0, spot, u1, v1, ug1, vg.at[0], (own1, a1s, a1r, b1s, b1r, c1s, c1r, w1s, w1r))
    g3 = Gather(2, spot, u3, v3, ug3, vg.at[1], (own3, a3s, a3r, b3s, b3r, c3s, c3r, w3s, w3r))
    gathers = (g1, None, g3)
    leaf = z * 4 + y

    def peer(dy):
        return device(z, lax.rem(y + dy, 4), q, c)

    def picked_from(f, j, i):
        row = one_ref[f, 4 * z + i] - leaf * 8
        col = one_ref[f, 4 * q + j] - e * 16
        here = (row >= 0) & (row < 8) & (col >= 0) & (col < 16)
        return (
            jnp.minimum(jnp.maximum(col, 0), 15),
            jnp.minimum(jnp.maximum(row, 0), 7),
            jnp.where(here, 1.0, 0.0),
        )

    def chosen_block(depth, m):
        ids = (two_ref, three_ref, four_ref)[depth]
        quarter = m // 2
        block = ids[leaf // (4 >> depth), 4 * quarter + 2 + m % 2] - 6 * quarter - 2
        return jnp.minimum(jnp.maximum(block, 0), 3)

    def member_block(m, a):
        return 4 * (m // 2) + 2 * lax.rem(a, 2) + a // 2

    barrier = pltpu.get_barrier_semaphore()

    def signal(dev):
        pl.semaphore_signal(barrier, inc=1, device_id=dev, device_id_type=MESH)

    mine_f = z // 2

    def u2_own_copy():
        return pltpu.make_async_copy(u2, u2v.at[c], u2_own.at[0])

    def v2_own_copy():
        return pltpu.make_async_copy(v2.at[block_at(c, BS), :], sq.at[:, block_at(y, 256)], u2_own.at[1])

    def u2_push():
        return remote(u2, u2v.at[c], u2_s, u2_r, partner)

    def u4_push(unit):
        rows = pl.ds(unit * UNIT, UNIT)
        return remote(u4.at[rows, :], ug4.at[rows, :], c4s.at[unit], c4r.at[unit], partner)

    def v4_copy():
        return pltpu.make_async_copy(v4.at[block_at(c, BS), :], acc.at[1], v4_sem)

    def enter():
        g1.begin()
        g3.begin()
        u2_own_copy().start()
        v2_own_copy().start()
        for t in range(8):

            @pl.when(t != e)
            def _():
                signal(device(z, y, t // 2, t % 2))

        for d in range(1, 8):
            member, base = g1.peer(d)
            signal(g1.leaf(member, base))
        for p in range(4):
            for r in range(2):
                j = 2 * r + c

                @pl.when(jnp.logical_not((p == z) & (j == y) & (mine_f == c)))
                def _():
                    signal(device(p, j, q, mine_f))

        own = (mine_f == c) & (y % 2 == c)
        pl.semaphore_wait(barrier, jnp.where(own, 21, 22))

        g1.send()

        u2_push().start()

        for unit in range(4):
            u4_push(unit).start()
        v4_copy().start()

    def split_update(depth, uhi, ulo, start, stop):
        def unit_of(n):
            k = n // 2
            step = jnp.where(k == 0, 0, jnp.where(k == 1, 3, jnp.where(k == 2, 1, 2)))
            return lax.rem(q + step, 4), lax.rem(n + c, 2)

        def fetch(n, slot):
            unit, half = unit_of(n)
            rows = pl.ds(pl.multiple_of(unit * UNIT, UNIT), UNIT)
            if depth < 3:
                pltpu.make_async_copy(
                    gathers[depth].ug.at[half, rows, :], stage.at[slot], stage_sem.at[slot]
                ).start()
            else:

                @pl.when(half == c)
                def _():
                    pltpu.make_async_copy(u4.at[rows, :], stage.at[slot], stage_sem.at[slot]).start()

                @pl.when(half != c)
                def _():
                    pltpu.make_async_copy(ug4.at[rows, :], stage.at[slot], stage_sem.at[slot]).start()

        def arrived(n):
            unit, half = unit_of(n)

            @pl.when(half != c)
            def _():
                if depth < 3:
                    gathers[depth].wait_other(unit)
                else:
                    rows = pl.ds(pl.multiple_of(unit * UNIT, UNIT), UNIT)
                    remote(
                        ug4.at[rows, :], ug4.at[rows, :], c4s.at[unit], c4r.at[unit], partner
                    ).wait_recv()

        def step(n, carry):
            slot = lax.rem(n, 2)

            @pl.when(n + 1 < stop)
            def _():
                arrived(n + 1)
                fetch(n + 1, 1 - slot)

            pltpu.make_async_copy(
                u4.at[pl.ds(0, UNIT), :], stage.at[slot], stage_sem.at[slot]
            ).wait()
            unit, half = unit_of(n)
            for i in range(2):
                block = half * 8 + unit * 2 + i
                quarter, j = block // 4, lax.rem(block, 4)
                to = (2 * quarter + lax.rem(j, 2)) * 2 + j // 2
                hi, lo = halves(stage[slot, i * BS : i * BS + BS, :])
                uhi[block_at(to, BS), :] = hi
                ulo[block_at(to, BS), :] = lo
            return carry

        arrived(start)
        fetch(start, start % 2)
        lax.fori_loop(start, stop, step, 0)

    def take(rootv, picked):
        def root_copy(j):
            return pltpu.make_async_copy(
                root_ref.at[:, :, j * BS : j * BS + BS], rootv.at[j], root_sem.at[j]
            )

        for j in range(16):
            root_copy(j).start()
        enter()
        for j in range(16):
            root_copy(j).wait()

        def pick(n, carry):
            f, j = n // 4, n % 4
            for i in range(4):
                col, row, here = picked_from(f, j, i)
                picked[f, j, i % 2 * 2 + i // 2] = (rootv[col, row] * here).T
            return carry

        lax.fori_loop(0, 8, pick, 0)
        core = remote(picked.at[1 - c], core_in, core_s, core_r, partner)
        core.start()
        core.wait()
        mine[...] = picked[c] + core_in[...]

    pl.run_scoped(
        take, pltpu.VMEM((16, 8, BS, BS), F32), pltpu.VMEM((2, 4, 4, BS, BS), F32)
    )

    def y_copy(d):
        to = lax.rem(y + d, 4)
        return remote(mine.at[to], y_in.at[d - 1], ys.at[d - 1], yr.at[d - 1], device(z, to, q, c))

    for d in (2, 1, 3):
        y_copy(d).start()
    g1.share_out()
    for d in (1, 3, 2):
        y_copy(d).wait()
    ready[...] = mine[y] + y_in[0] + y_in[1] + y_in[2]

    def h_copy(k, d):
        return remote(
            ready, held.at[y // 2, pl.ds(4 * z, 4)], h_s.at[k * 4 + d], h_r.at[z * 2 + y // 2],
            device(2 * c + k, lax.rem(y + d, 4), q, y % 2),
        )

    def to_self(k):
        return (2 * c + k == z) & (y % 2 == c)

    for d in (2, 1, 3):
        for k in range(2):
            h_copy(k, d).start()
    for k in range(2):

        @pl.when(jnp.logical_not(to_self(k)))
        def _():
            h_copy(k, 0).start()

        @pl.when(to_self(k))
        def _():
            held[y // 2, pl.ds(4 * z, 4)] = ready[...]

    u2_own_copy().wait()
    u2_push().wait()

    def split_two(b, carry):
        m = b // 2
        src = 4 * (m // 2) + 2 * lax.rem(b, 2) + lax.rem(m, 2)
        hi, lo = halves(u2v[src // 8, block_at(lax.rem(src, 8), BS), :])
        u2hi[block_at(b, BS), :] = hi
        u2lo[block_at(b, BS), :] = lo
        return carry

    lax.fori_loop(0, 16, split_two, 0)
    g1.forward()
    split_update(0, uhi0, ulo0, 0, 6)
    for p in range(4):
        for r in range(2):

            @pl.when(jnp.logical_not((p == z) & (2 * r + c == y) & (mine_f == c)))
            def _():
                there = held.at[r, pl.ds(4 * p, 4)]
                remote(there, there, h_s.at[0], h_r.at[p * 2 + r], partner).wait_recv()

    for d in (2, 1, 3):
        for k in range(2):
            h_copy(k, d).wait_send()
    for k in range(2):

        @pl.when(jnp.logical_not(to_self(k)))
        def _():
            h_copy(k, 0).wait_send()

    def pair_copy(ref, at, r, s_sem, r_sem):
        return remote(
            ref.at[2 * r + c], ref.at[2 * r + c], s_sem.at[at, r], r_sem.at[at, r], partner
        )

    def pair_arrived(ref, at, r, s_sem, r_sem):
        there = ref.at[2 * r + 1 - c]
        return remote(there, there, s_sem.at[at, r], r_sem.at[at, r], partner)

    def begin_level(at):
        hq = (hq0, hq1)[at]
        for r in range(2):
            for b in range(16):
                value = held[r, b]
                hi, lo = halves(value)
                hs[r * BS : r * BS + BS, b * BS : b * BS + BS] = hi
                hs[256 + r * BS : 256 + r * BS + BS, b * BS : b * BS + BS] = lo
                hq[2 * r + c, b] = value
            pair_copy(hq, at, r, hx_s, hx_r).start()

    def piece_copy(at, to):
        return remote(
            st.at[to], (ptl0, ptl1)[at].at[pl.ds(2 * e, 2)], ps.at[to], pr.at[at, e],
            device(z, y, to // 2, lax.rem(to, 2)),
        )

    def give(at, to, turned):
        ptl = (ptl0, ptl1)[at]

        @pl.when(to == e)
        def _():
            for r in range(2):
                ptl[2 * e + r] = turned[r]

        @pl.when(to != e)
        def _():
            for r in range(2):
                st[to, r] = turned[r]
            piece_copy(at, to).start()

    def part_copy(at, to, r):
        return remote(
            st.at[to, r], (ptl0, ptl1)[at].at[2 * e + r], psr.at[to, r], prr.at[e, r],
            device(z, y, to // 2, lax.rem(to, 2)),
        )

    def give_part(at, to, r, turned):
        ptl = (ptl0, ptl1)[at]

        @pl.when(to == e)
        def _():
            ptl[2 * e + r] = turned

        @pl.when(to != e)
        def _():
            st[to, r] = turned
            part_copy(at, to, r).start()

    def square_loop(at, out, cols, uhi, ulo, parts):
        ptl = (ptl0, ptl1)[at]

        def square_step(s, carry):
            k = s // 2
            step = jnp.where(k == 0, 0, jnp.where(k == 1, 1, jnp.where(k == 2, 3, 2)))
            m = 2 * lax.rem(q + step, 4) + lax.rem(s + c, 2)

            @pl.when(m != e)
            def _():
                if parts:
                    for r in range(2):
                        there = ptl.at[2 * m + r]
                        remote(there, there, psr.at[m, r], prr.at[m, r], partner).wait_recv()
                else:
                    there = ptl.at[pl.ds(2 * m, 2)]
                    remote(there, there, ps.at[m], pr.at[at, m], partner).wait_recv()

            hi, lo = halves(jnp.concatenate([ptl[2 * m], ptl[2 * m + 1]], 1))
            rows = block_at(m, 256)
            both = dot(jnp.concatenate([hi, lo], 0), uhi[rows, :])
            out[:, cols] += both[:BS] + both[BS:] + dot(hi, ulo[rows, :])
            return carry

        lax.fori_loop(0, 8, square_step, 0)

    def next_held(depth, at, square):
        hq, pq, ptl = ((hq0, pq0, ptl0), (hq1, pq1, ptl1))[at]
        for r in range(2):
            pair_arrived(hq, at, r, hx_s, hx_r).wait_recv()
            pair_arrived(pq, at, r, px_s, px_r).wait_recv()
        chosen = chosen_block(depth, e)
        for m in range(8):
            block = member_block(m, chosen_block(depth, m))
            held[0, 2 * m] = square[:, m * BS : m * BS + BS]
            held[0, 2 * m + 1] = -ptl[block]
            held[1, 2 * m] = -pq[chosen, :, m * BS : m * BS + BS]
            held[1, 2 * m + 1] = hq[chosen, block]

    def end_level(at, parts):
        hq, pq = ((hq0, pq0), (hq1, pq1))[at]
        for r in range(2):
            pair_copy(hq, at, r, hx_s, hx_r).wait_send()
            pair_copy(pq, at, r, px_s, px_r).wait_send()

        def sent(to, carry):
            @pl.when(to != e)
            def _():
                if parts:
                    for r in range(2):
                        part_copy(at, to, r).wait_send()
                else:
                    piece_copy(at, to).wait_send()

            return carry

        lax.fori_loop(0, 8, sent, 0)

    def level_two(later):
        pq = pq1
        begin_level(1)
        cols = block_at(y, 256)
        both = dot(hs[...], u2hi[...])
        part = both[:256] + both[256:] + dot(hs[:256, :], u2lo[...])

        def panel_out(dy, r):
            rows = pq.at[2 * r + c, :, cols]
            return remote(rows, rows, ag_s.at[dy, r], ag_r.at[y, r], peer(dy))

        def turn(m, r):
            for core in range(2):
                value = pq[2 * r + c, :, pl.ds(pl.multiple_of(m * 256 + core * BS, BS), BS)]
                give_part(1, 2 * m + core, r, value.T)

        for r in range(2):
            pq[2 * r + c, :, cols] = part[r * BS : r * BS + BS]
        for dy in (1, 3, 2):
            panel_out(dy, 0).start()
        turn(y, 0)
        turn(y, 1)
        for dy in (1, 3, 2):
            panel_out(dy, 0).wait_send()
        for dy in (1, 3, 2):
            panel_out(dy, 1).start()
        for r in range(2):
            for dy in (1, 3, 2):
                m = lax.rem(y + dy, 4)
                there = pq.at[2 * r + c, :, block_at(m, 256)]
                remote(there, there, ag_s.at[0, r], ag_r.at[m, r], partner).wait_recv()
                turn(m, r)
        for r in range(2):
            pair_copy(pq, 1, r, px_s, px_r).start()
        g3.forward()
        v2_own_copy().wait()
        square_loop(1, sq, cols, u2hi, u2lo, True)

        def square_out(dy):
            return remote(sq.at[:, cols], sq.at[:, cols], sg_s.at[dy], sg_r.at[y], peer(dy))

        for dy in (1, 3, 2):
            square_out(dy).start()
        later()
        for dy in (1, 3, 2):
            panel_out(dy, 1).wait_send()
            m = lax.rem(y + dy, 4)
            there = sq.at[:, block_at(m, 256)]
            remote(there, there, sg_s.at[0], sg_r.at[m], partner).wait_recv()
        next_held(1, 1, sq)
        for dy in (1, 3, 2):
            square_out(dy).wait_send()
        end_level(1, True)

    def level(depth, uhi, ulo, early, meanwhile):
        last = depth == 3
        at = depth % 2
        hq, pq, ptl = ((hq0, pq0, ptl0), (hq1, pq1, ptl1))[at]
        begin_level(at)
        early()

        def panel_step(k, carry):
            step = jnp.where(k == 0, 2, jnp.where(k == 1, 1, jnp.where(k == 2, 3, 0)))
            t = lax.rem(q + step, 4)
            cols = block_at(t, 256)
            both = dot(hs[...], uhi[:, cols])
            part = both[:256] + both[256:] + dot(hs[:256, :], ulo[:, cols])
            for r in range(2):
                pq[2 * r + c, :, cols] = part[r * BS : r * BS + BS]
            for core in range(2):
                turned = [
                    part[r * BS : r * BS + BS, core * BS : core * BS + BS].T for r in range(2)
                ]
                give(at, 2 * t + core, turned)
            return carry

        lax.fori_loop(0, 4, panel_step, 0)
        for r in range(2):
            pair_copy(pq, at, r, px_s, px_r).start()
        meanwhile()
        if last:
            v4_copy().wait()
            acc[0] = acc[1]
        else:
            gathers[depth].collect_pivot()
            acc[0] = vg[depth // 2]
        square_loop(at, acc.at[0], slice(None), uhi, ulo, False)
        if not last:
            next_held(depth, at, acc.at[0])
        else:
            for r in range(2):
                pair_arrived(hq, at, r, hx_s, hx_r).wait_recv()
                pair_arrived(pq, at, r, px_s, px_r).wait_recv()

            def rows_of(half):
                for p in range(2):
                    quarter = 2 * half + p
                    yield p * 768, acc[0, :, block_at(quarter, 256)]
                    for a in range(4):
                        yield p * 768 + 256 + a * BS, -ptl[2 * (2 * quarter + a % 2) + a // 2]

            for to, value in rows_of(1 - c):
                xin[1, :, to : to + value.shape[1]] = value
            cross = remote(xin.at[1], xin.at[0], xs_s, xs_r, partner)
            cross.start()
            for to, value in rows_of(c):
                out_ref[0, block_at(c, BS), to : to + value.shape[1]] = value
            for a in range(4):
                rows = slice(256 + a * BS, 256 + a * BS + BS)
                for p in range(2):
                    quarter = 2 * c + p
                    out_ref[0, rows, p * 768 : p * 768 + 256] = -pq[a, :, block_at(quarter, 256)]
                    for b in range(4):
                        block = 2 * (2 * quarter + b % 2) + b // 2
                        to = p * 768 + 256 + b * BS
                        out_ref[0, rows, to : to + BS] = hq[a, block]
            cross.wait()
            out_ref[0, block_at(1 - c, BS), :] = xin[0]

        end_level(at, False)

    def levels(uhi1, ulo1):
        def rest_of_one():
            g1.collect()
            split_update(0, uhi0, ulo0, 6, 8)

        def three():
            g3.collect()
            split_update(2, uhi1, ulo1, 0, 8)

        g1.send_pivot()
        g3.send()
        g3.send_pivot()
        level(0, uhi0, ulo0, rest_of_one, lambda: None)
        g3.share_out()
        level_two(three)
        level(2, uhi1, ulo1, lambda: None, lambda: split_update(3, uhi0, ulo0, 0, 8))
        level(3, uhi0, ulo0, lambda: None, lambda: None)

    pl.run_scoped(levels, pltpu.VMEM((ANC, SEP), BF16), pltpu.VMEM((ANC, SEP), BF16))
    g1.finish()
    g3.finish()
    for unit in range(4):
        u4_push(unit).wait_send()


def whole(blocks, root, updates, pivots):
    dma = pltpu.SemaphoreType.DMA
    any_space = pl.BlockSpec(memory_space=pl.ANY)
    smem = pl.BlockSpec(memory_space=pltpu.SMEM)
    gather_sems = []
    for n in (8, 2):
        gather_sems += [
            dma((2,)), dma((n,)), dma((n,)), dma((4, n)), dma((4, n)), dma((4,)), dma((4,)), dma((n,)), dma((n,)),
        ]
    outs = pl.pallas_call(
        whole_kernel,
        out_shape=[jax.ShapeDtypeStruct((1, 768, 1536), F32)]
        + [jax.ShapeDtypeStruct((2, 1024, 1024), F32)] * 2
        + [jax.ShapeDtypeStruct((1024, 1024), F32)],
        in_specs=[smem] * 4 + [any_space] * 9,
        out_specs=[pl.BlockSpec(memory_space=pltpu.VMEM)] + [any_space] * 3,
        scratch_shapes=[
            pltpu.VMEM((4, 4, BS, BS), F32),
            pltpu.VMEM((4, 4, BS, BS), F32),
            pltpu.VMEM((3, 4, BS, BS), F32),
            pltpu.VMEM((4, BS, BS), F32),
            pltpu.VMEM((2, 16, BS, BS), F32),
            pltpu.VMEM((4, 16, BS, BS), F32),
            pltpu.VMEM((4, 16, BS, BS), F32),
            pltpu.VMEM((4, BS, SEP), F32),
            pltpu.VMEM((4, BS, SEP), F32),
            pltpu.VMEM((16, BS, BS), F32),
            pltpu.VMEM((16, BS, BS), F32),
            pltpu.VMEM((2, 1024, 256), F32),
            pltpu.VMEM((ANC, 256), BF16),
            pltpu.VMEM((ANC, 256), BF16),
            pltpu.VMEM((ANC, SEP), BF16),
            pltpu.VMEM((ANC, SEP), BF16),
            pltpu.VMEM((2, UNIT, SEP), F32),
            pltpu.VMEM((512, ANC), BF16),
            pltpu.VMEM((8, 2, BS, BS), F32),
            pltpu.VMEM((2, BS, SEP), F32),
            pltpu.VMEM((2, BS, SEP), F32),
            pltpu.VMEM((BS, SEP), F32),
            pltpu.VMEM((2, BS, 1536), F32),
            dma((16,)),
            dma,
            dma,
            dma((3,)),
            dma((3,)),
            dma((8,)),
            dma((8,)),
        ]
        + gather_sems
        + [
            dma((4,)),
            dma((4,)),
            dma,
            dma((2,)),
            dma,
            dma,
            dma((4, 2)),
            dma((4, 2)),
            dma((4,)),
            dma((4,)),
            dma((2,)),
            dma((8,)),
            dma((2, 8)),
            dma((8, 2)),
            dma((8, 2)),
            dma((2, 2)),
            dma((2, 2)),
            dma((2, 2)),
            dma((2, 2)),
            dma,
            dma,
        ],
        compiler_params=pltpu.CompilerParams(
            collective_id=0, has_side_effects=True, vmem_limit_bytes=60 * 2**20
        ),
        name="whole",
    )(*blocks, root, *updates, *pivots)
    return outs[0]


def shards(
    root_inverse,
    blocks_one,
    blocks_two,
    blocks_three,
    blocks_four,
    update_one,
    update_two,
    update_three,
    update_four,
    pivot_one,
    pivot_two,
    pivot_three,
    pivot_four,
):
    return whole(
        (blocks_one, blocks_two, blocks_three, blocks_four),
        root_inverse.reshape(8, BS, 2048),
        (update_one, update_two, update_three, update_four),
        (pivot_one, pivot_two, pivot_three, pivot_four),
    )


def solution(mesh):
    mesh = Mesh(mesh.devices.reshape(2, 2, 2, 2, 4, 2), AXES)
    leaf = AXES[:4]
    placed = (
        P(leaf, ("row", "col")),
        P(),
        P(),
        P(),
        P(),
        P("col", leaf),
        P("col", leaf),
        P("col", leaf),
        P("col", leaf),
        P("row", leaf),
        P("row", leaf),
        P("row", leaf),
        P("row", leaf),
    )
    return jax.shard_map(
        shards, mesh=mesh, in_specs=placed, out_specs=P(leaf, "row", "col"), check_vma=False
    )
```

time: 223 us -> 170 us (0.76)
  Pallas kernels: 211 us -> 164 us
  local copies, waits for them, and re-layouts: 8.55 us -> 4.84 us
  other arithmetic: 2.41 us -> 0 us
    pallas_call x1, Pallas kernels: 211 us -> 164 us  [whole(): pl.pallas_call(whole_kernel, out_shape=[jax.ShapeDtypeStruct((1, 768, 153...]
    unnamed x3 -> x1, local copies, waits for them, and re-layouts: 5.54 us -> 4.84 us
where the time goes in v3:
time: 170 us; the launch traced here: 169 us
  Pallas kernels  164 us (96%)
  local copies, waits for them, and re-layouts  4.84 us (3%)
    pallas_call x1, Pallas kernels, whole(): pl.pallas_call(whole_kernel, out_shape=[jax.ShapeDtypeStruct((1, 768, 153...  164 us
    unnamed x1, local copies, waits for them, and re-layouts  4.84 us

profile of v3, /device:TPU:1, one launch (start us, length us, event | category | flops | bytes accessed | tf_op | source)
XLA Modules:
  0.0 168.5 jit_solution(11833503194441213598)
XLA Ops:
  0.0 163.7 %whole.1 = (f32[1,768,1536]{2,1,0:T(8,128)}, f32[2,1024,1024]{2,1,0:T(8,128)}, f32[2,1024,1024]{2,1,0:T(8,128)}, f32[1024,1024]{1,0:T(8,128)}) custom-call(s32[2,16]{1,0:T(2,128)} %one_ref.1, s32[4,16]{1,0:T(4,128)} %two_ref.1, s32[8,16]{1,0:T(8,128)} %three_ref.1, s32[16,16]{1,0:T(8,128)} %four_ref.1, f32[8,128,2048]{2,1,0:T(8,128)} %bitcast.1, ...), custom_call_target="tpu_custom_call" | custom-call | tf_op jit(solution)/shard_map/whole/pallas_call | solution.py:729
  163.7 4.8 %copy.15 = f32[1,768,1536]{2,1,0:T(8,128)} copy(f32[1,768,1536]{2,1,0:T(8,128)} %get-tuple-element.6) | data formatting | bytes 9437184

commit v4 on v3

--- a/solution.py
+++ b/solution.py
@@ -69,12 +69,16 @@
     def rows(self, first, units):
         return pl.ds(pl.multiple_of(first * UNIT, UNIT), units * UNIT)
 
-    def own(self):
-        return (
-            pltpu.make_async_copy(self.u, self.ug.at[self.c, :, self.cols(self.me)], self.own_sem.at[0]),
-            pltpu.make_async_copy(
-                self.v.at[block_at(self.c, BS), :], self.vg.at[:, self.cols(self.me)], self.own_sem.at[1]
-            ),
+    def load(self, buffer):
+        return pltpu.make_async_copy(self.u, buffer, self.own_sem.at[0])
+
+    def store(self, buffer):
+        there = self.ug.at[self.c, :, self.cols(self.me)]
+        return pltpu.make_async_copy(buffer, there, self.own_sem.at[0])
+
+    def own_pivot(self):
+        return pltpu.make_async_copy(
+            self.v.at[block_at(self.c, BS), :], self.vg.at[:, self.cols(self.me)], self.own_sem.at[1]
         )
 
     def a_copy(self, d):
@@ -127,9 +131,9 @@
             there, there, self.c_s.at[unit], self.c_r.at[unit], device(self.z, self.y, self.x, 1 - self.c)
         )
 
-    def begin(self):
-        for copy in self.own():
-            copy.start()
+    def begin(self, buffer):
+        self.load(buffer).start()
+        self.own_pivot().start()
 
     def send(self):
         for d in range(1, self.count):
@@ -147,9 +151,6 @@
         lax.fori_loop(1, self.count, step, 0)
 
     def share_out(self):
-        for copy in self.own():
-            copy.wait()
-
         def body(member):
             self.a_arrived(member).wait_recv()
             for n in range(2):
@@ -177,6 +178,8 @@
         self.c_copy(lax.rem(self.x + 2, 4), self.c).start()
 
     def collect_pivot(self):
+        self.own_pivot().wait()
+
         def step(d, carry):
             self.v_arrived(lax.rem(self.me + self.count - d, self.count)).wait_recv()
             return carry
@@ -207,12 +210,12 @@
     one_ref, two_ref, three_ref, four_ref, root_ref, u1, u2, u3, u4, v1, v2, v3, v4,
     out_ref, ug1, ug3, ug4,
     core_in, mine, y_in, ready, held, hq0, hq1, pq0, pq1, ptl0, ptl1,
-    u2v, u2hi, u2lo, uhi0, ulo0, stage, hs, st, vg, acc, sq, xin,
+    u2v, u2hi, u2lo, uhi0, ulo0, stage, hs, st, vg, acc, sq, xin, outv,
     root_sem, core_s, core_r, ys, yr, h_s, h_r,
     own1, a1s, a1r, b1s, b1r, c1s, c1r, w1s, w1r,
     own3, a3s, a3r, b3s, b3r, c3s, c3r, w3s, w3r,
     c4s, c4r, v4_sem, u2_own, u2_s, u2_r, ag_s, ag_r, sg_s, sg_r,
-    stage_sem, ps, pr, psr, prr, hx_s, hx_r, px_s, px_r, xs_s, xs_r,
+    stage_sem, ps, pr, psr, prr, hx_s, hx_r, px_s, px_r, xs_s, xs_r, out_sem,
 ):
     spot = place()
     z, y, q, c = spot
@@ -268,9 +271,11 @@
     def v4_copy():
         return pltpu.make_async_copy(v4.at[block_at(c, BS), :], acc.at[1], v4_sem)
 
-    def enter():
-        g1.begin()
-        g3.begin()
+    travelling = (g1, g3)
+
+    def enter(buffers):
+        for g, buffer in zip(travelling, buffers):
+            g.begin(buffer)
         u2_own_copy().start()
         v2_own_copy().start()
         for t in range(8):
@@ -362,7 +367,7 @@
         fetch(start, start % 2)
         lax.fori_loop(start, stop, step, 0)
 
-    def take(rootv, picked):
+    def take(rootv, picked, *buffers):
         def root_copy(j):
             return pltpu.make_async_copy(
                 root_ref.at[:, :, j * BS : j * BS + BS], rootv.at[j], root_sem.at[j]
@@ -370,7 +375,10 @@
 
         for j in range(16):
             root_copy(j).start()
-        enter()
+        enter(buffers)
+        for g, buffer in zip(travelling, buffers):
+            g.load(buffer).wait()
+            g.store(buffer).start()
         for j in range(16):
             root_copy(j).wait()
 
@@ -386,9 +394,15 @@
         core.start()
         core.wait()
         mine[...] = picked[c] + core_in[...]
+        for g, buffer in zip(travelling, buffers):
+            g.store(buffer).wait()
 
     pl.run_scoped(
-        take, pltpu.VMEM((16, 8, BS, BS), F32), pltpu.VMEM((2, 4, 4, BS, BS), F32)
+        take,
+        pltpu.VMEM((16, 8, BS, BS), F32),
+        pltpu.VMEM((2, 4, 4, BS, BS), F32),
+        pltpu.VMEM((1024, 128), F32),
+        pltpu.VMEM((1024, 512), F32),
     )
 
     def y_copy(d):
@@ -625,6 +639,11 @@
             square_out(dy).wait_send()
         end_level(1, True)
 
+    def out_copy(first, rows):
+        return pltpu.make_async_copy(
+            outv.at[pl.ds(first, rows), :], out_ref.at[0, pl.ds(first, rows), :], out_sem.at[min(first, 1)]
+        )
+
     def level(depth, uhi, ulo, early, meanwhile):
         last = depth == 3
         at = depth % 2
@@ -654,6 +673,19 @@
         if last:
             v4_copy().wait()
             acc[0] = acc[1]
+            for r in range(2):
+                pair_arrived(hq, at, r, hx_s, hx_r).wait_recv()
+                pair_arrived(pq, at, r, px_s, px_r).wait_recv()
+            for a in range(4):
+                rows = slice(256 + a * BS, 256 + a * BS + BS)
+                for p in range(2):
+                    quarter = 2 * c + p
+                    outv[rows, p * 768 : p * 768 + 256] = -pq[a, :, block_at(quarter, 256)]
+                    for b in range(4):
+                        block = 2 * (2 * quarter + b % 2) + b // 2
+                        to = p * 768 + 256 + b * BS
+                        outv[rows, to : to + BS] = hq[a, block]
+            out_copy(256, 512).start()
         else:
             gathers[depth].collect_pivot()
             acc[0] = vg[depth // 2]
@@ -661,9 +693,6 @@
         if not last:
             next_held(depth, at, acc.at[0])
         else:
-            for r in range(2):
-                pair_arrived(hq, at, r, hx_s, hx_r).wait_recv()
-                pair_arrived(pq, at, r, px_s, px_r).wait_recv()
 
             def rows_of(half):
                 for p in range(2):
@@ -677,18 +706,12 @@
             cross = remote(xin.at[1], xin.at[0], xs_s, xs_r, partner)
             cross.start()
             for to, value in rows_of(c):
-                out_ref[0, block_at(c, BS), to : to + value.shape[1]] = value
-            for a in range(4):
-                rows = slice(256 + a * BS, 256 + a * BS + BS)
-                for p in range(2):
-                    quarter = 2 * c + p
-                    out_ref[0, rows, p * 768 : p * 768 + 256] = -pq[a, :, block_at(quarter, 256)]
-                    for b in range(4):
-                        block = 2 * (2 * quarter + b % 2) + b // 2
-                        to = p * 768 + 256 + b * BS
-                        out_ref[0, rows, to : to + BS] = hq[a, block]
+                outv[block_at(c, BS), to : to + value.shape[1]] = value
             cross.wait()
-            out_ref[0, block_at(1 - c, BS), :] = xin[0]
+            outv[block_at(1 - c, BS), :] = xin[0]
+            out_copy(0, 256).start()
+            out_copy(0, 256).wait()
+            out_copy(256, 512).wait()
 
         end_level(at, False)
 
@@ -732,7 +755,7 @@
         + [jax.ShapeDtypeStruct((2, 1024, 1024), F32)] * 2
         + [jax.ShapeDtypeStruct((1024, 1024), F32)],
         in_specs=[smem] * 4 + [any_space] * 9,
-        out_specs=[pl.BlockSpec(memory_space=pltpu.VMEM)] + [any_space] * 3,
+        out_specs=[any_space] * 4,
         scratch_shapes=[
             pltpu.VMEM((4, 4, BS, BS), F32),
             pltpu.VMEM((4, 4, BS, BS), F32),
@@ -757,6 +780,7 @@
             pltpu.VMEM((2, BS, SEP), F32),
             pltpu.VMEM((BS, SEP), F32),
             pltpu.VMEM((2, BS, 1536), F32),
+            pltpu.VMEM((768, 1536), F32),
             dma((16,)),
             dma,
             dma,
@@ -788,6 +812,7 @@
             dma((2, 2)),
             dma,
             dma,
+            dma((2,)),
         ],
         compiler_params=pltpu.CompilerParams(
             collective_id=0, has_side_effects=True, vmem_limit_bytes=60 * 2**20

time: 170 us -> 168 us (0.988)
  no operation moved by 1% of the time
where the time goes in v4:
time: 168 us
  Pallas kernels  163 us (97%)
  local copies, waits for them, and re-layouts  4.84 us (3%)
    pallas_call x1, Pallas kernels, whole(): pl.pallas_call(whole_kernel, out_shape=[jax.ShapeDtypeStruct((1, 768, 153...  163 us
    unnamed x1, local copies, waits for them, and re-layouts  4.84 us

profile of v4, /device:TPU:1, one launch (start us, length us, event | category | flops | bytes accessed | tf_op | source)
XLA Modules:
  0.0 167.6 jit_solution(13939033531924561855)
XLA Ops:
  0.0 162.7 %whole.1 = (f32[1,768,1536]{2,1,0:T(8,128)}, f32[2,1024,1024]{2,1,0:T(8,128)}, f32[2,1024,1024]{2,1,0:T(8,128)}, f32[1024,1024]{1,0:T(8,128)}) custom-call(s32[2,16]{1,0:T(2,128)} %one_ref.1, s32[4,16]{1,0:T(4,128)} %two_ref.1, s32[8,16]{1,0:T(8,128)} %three_ref.1, s32[16,16]{1,0:T(8,128)} %four_ref.1, f32[8,128,2048]{2,1,0:T(8,128)} %bitcast.1, ...), custom_call_target="tpu_custom_call" | custom-call | tf_op jit(solution)/shard_map/whole/pallas_call | solution.py:752
  162.7 4.8 %copy.15 = f32[1,768,1536]{2,1,0:T(8,128)} copy(f32[1,768,1536]{2,1,0:T(8,128)} %get-tuple-element.6) | data formatting | bytes 9437184

commit v5 on v4

--- a/solution.py
+++ b/solution.py
@@ -459,15 +459,6 @@
             def _():
                 there = held.at[r, pl.ds(4 * p, 4)]
                 remote(there, there, h_s.at[0], h_r.at[p * 2 + r], partner).wait_recv()
-
-    for d in (2, 1, 3):
-        for k in range(2):
-            h_copy(k, d).wait_send()
-    for k in range(2):
-
-        @pl.when(jnp.logical_not(to_self(k)))
-        def _():
-            h_copy(k, 0).wait_send()
 
     def pair_copy(ref, at, r, s_sem, r_sem):
         return remote(
@@ -734,6 +725,15 @@
         level(3, uhi0, ulo0, lambda: None, lambda: None)
 
     pl.run_scoped(levels, pltpu.VMEM((ANC, SEP), BF16), pltpu.VMEM((ANC, SEP), BF16))
+    for d in (2, 1, 3):
+        for k in range(2):
+            h_copy(k, d).wait_send()
+    for k in range(2):
+
+        @pl.when(jnp.logical_not(to_self(k)))
+        def _():
+            h_copy(k, 0).wait_send()
+
     g1.finish()
     g3.finish()
     for unit in range(4):

time: 168 us -> 168 us (level)
  no operation moved by 1% of the time
where the time goes in v5:
time: 168 us; the launch traced here: 167 us
  Pallas kernels  162 us (96%)
  local copies, waits for them, and re-layouts  4.84 us (3%)
    pallas_call x1, Pallas kernels, whole(): pl.pallas_call(whole_kernel, out_shape=[jax.ShapeDtypeStruct((1, 768, 153...  162 us
    unnamed x1, local copies, waits for them, and re-layouts  4.84 us

profile of v5, /device:TPU:1, one launch (start us, length us, event | category | flops | bytes accessed | tf_op | source)
XLA Modules:
  0.0 167.3 jit_solution(16088635051245627111)
XLA Ops:
  0.0 162.4 %whole.1 = (f32[1,768,1536]{2,1,0:T(8,128)}, f32[2,1024,1024]{2,1,0:T(8,128)}, f32[2,1024,1024]{2,1,0:T(8,128)}, f32[1024,1024]{1,0:T(8,128)}) custom-call(s32[2,16]{1,0:T(2,128)} %one_ref.1, s32[4,16]{1,0:T(4,128)} %two_ref.1, s32[8,16]{1,0:T(8,128)} %three_ref.1, s32[16,16]{1,0:T(8,128)} %four_ref.1, f32[8,128,2048]{2,1,0:T(8,128)} %bitcast.1, ...), custom_call_target="tpu_custom_call" | custom-call | tf_op jit(solution)/shard_map/whole/pallas_call | solution.py:752
  162.4 4.8 %copy.15 = f32[1,768,1536]{2,1,0:T(8,128)} copy(f32[1,768,1536]{2,1,0:T(8,128)} %get-tuple-element.6) | data formatting | bytes 9437184
